TPU v7x, 512 devices: a whole 4x4x16 slice. The times are simulated.
512 devices in a mesh: seq: 16 (over x_lo, y, core), tp: 32 (over x_hi, z).
Axes of the slice: x: 4 (x_hi: 2, x_lo: 2; x = x_hi * 2 + x_lo), y: 4, z: 16, core: 2. Of those that a mesh axis runs over, the one named last changes fastest.
Arguments:
- tokens: bfloat16 [1024, 8192], P('tp', 'seq'), may hold values from -6 to 6
- cotangent: bfloat16 [1024, 8192], P('tp', 'seq'), may hold values from -0.5 to 0.5
- gate_codes: bfloat16 [8192, 16384], P('seq', 'tp'), may hold values from -4 to 4
- gate_scales: float32 [64, 128], replicated, may hold values from 0.004 to 0.02
- up_codes: bfloat16 [8192, 16384], P('seq', 'tp'), may hold values from -4 to 4
- up_scales: float32 [64, 128], replicated, may hold values from 0.004 to 0.02
- down_codes: bfloat16 [16384, 8192], P('tp', 'seq'), may hold values from -4 to 4
- down_scales: float32 [128, 64], replicated, may hold values from 0.004 to 0.02
Outputs:
- mixed_out: bfloat16 [1024, 8192], P('tp', 'seq')
- grad_gate: float32 [8192, 16384], P('seq', 'tp')
- grad_up: float32 [8192, 16384], P('seq', 'tp')
- grad_down: float32 [16384, 8192], P('tp', 'seq')
All inputs are finite; a program needn't handle non-finite values.
Results may differ from a plain program's by a relative error of at most 0.04.
Values may be sent and summed in bfloat16 or wider, within the bound.
No kernel may reach another device: no remote copies, remote signals or barrier semaphores. Data moves between devices by JAX's collectives and lax.ppermute only.
A program may use at most 64 MiB of HBM per device.

v0:
```python
import jax
import jax.numpy as jnp
from jax import lax
from jax.sharding import PartitionSpec as P

BLOCK = 128


def block_scales(scales, row_first, row_count, col_first, col_count):
    row_ids = (row_first + jnp.arange(row_count, dtype=jnp.int32)) // BLOCK
    row_pick = (row_ids[:, None] == jnp.arange(scales.shape[0], dtype=jnp.int32)[None, :]).astype(
        jnp.float32
    )
    col_ids = (col_first + jnp.arange(col_count, dtype=jnp.int32)) // BLOCK
    col_pick = (jnp.arange(scales.shape[1], dtype=jnp.int32)[:, None] == col_ids[None, :]).astype(
        jnp.float32
    )
    picked = jnp.dot(row_pick, scales, precision=lax.Precision.HIGHEST)
    return jnp.dot(picked, col_pick, precision=lax.Precision.HIGHEST)


def dequantize(codes, scales, row_first, col_first):
    factors = block_scales(scales, row_first, codes.shape[0], col_first, codes.shape[1])
    return (codes.astype(jnp.float32) * factors).astype(jnp.bfloat16)


def gate_grads(hidden_grad, gate_sum, up_sum):
    sigma = jax.nn.sigmoid(gate_sum)
    gate_grad = (hidden_grad * up_sum * sigma * (1.0 + gate_sum * (1.0 - sigma))).astype(
        jnp.bfloat16
    )
    up_grad = (hidden_grad * jax.nn.silu(gate_sum)).astype(jnp.bfloat16)
    return (gate_grad, up_grad)


def back_product(rows_grad, w_down):
    return lax.dot_general(
        rows_grad, w_down, (((1,), (1,)), ((), ())), preferred_element_type=jnp.float32
    )


def on_device(
    tokens, cotangent, gate_codes, gate_scales, up_codes, up_scales, down_codes, down_scales
):
    seq_place = lax.axis_index("seq")
    tp_place = lax.axis_index("tp")
    width_rows = gate_codes.shape[0]
    unit_cols = gate_codes.shape[1]
    w_gate = dequantize(gate_codes, gate_scales, seq_place * width_rows, tp_place * unit_cols)
    w_up = dequantize(up_codes, up_scales, seq_place * width_rows, tp_place * unit_cols)
    w_down = dequantize(down_codes, down_scales, tp_place * unit_cols, seq_place * width_rows)
    frames, out_grads = (
        lax.all_gather(tokens, "tp", axis=0, tiled=True),
        lax.all_gather(cotangent, "tp", axis=0, tiled=True),
    )
    w_pair = jnp.concatenate([w_gate, w_up], axis=1)
    picked = frames
    totals = lax.psum(
        jnp.dot(picked, w_pair, preferred_element_type=jnp.float32).astype(jnp.bfloat16), "seq"
    ).astype(jnp.float32)
    gate_sum = totals[:, :unit_cols]
    up_sum = totals[:, unit_cols:]
    hidden = (jax.nn.silu(gate_sum) * up_sum).astype(jnp.bfloat16)
    picked = hidden
    mixed_out = lax.psum_scatter(
        jnp.dot(picked, w_down, preferred_element_type=jnp.float32).astype(jnp.bfloat16),
        "tp",
        scatter_dimension=0,
        tiled=True,
    )
    hidden_grad = lax.psum(back_product(out_grads, w_down).astype(jnp.bfloat16), "seq").astype(
        jnp.float32
    )
    gate_grad, up_grad = gate_grads(hidden_grad, gate_sum, up_sum)
    pair_grad = jnp.concatenate([gate_grad, up_grad], axis=1)
    weight_pair = lax.dot_general(
        frames, pair_grad, (((0,), (0,)), ((), ())), preferred_element_type=jnp.float32
    )
    grad_down = lax.dot_general(
        hidden, out_grads, (((0,), (0,)), ((), ())), preferred_element_type=jnp.float32
    )
    return (mixed_out, weight_pair[:, :unit_cols], weight_pair[:, unit_cols:], grad_down)


def solution(mesh):
    return jax.shard_map(
        on_device,
        mesh=mesh,
        in_specs=(
            P("tp", "seq"),
            P("tp", "seq"),
            P("seq", "tp"),
            P(),
            P("seq", "tp"),
            P(),
            P("tp", "seq"),
            P(),
        ),
        out_specs=(P("tp", "seq"), P("seq", "tp"), P("seq", "tp"), P("tp", "seq")),
        check_vma=False,
    )
```

profile of v0, /device:TPU:24, one launch (start us, length us, event | category | flops | bytes accessed | tf_op | source)
XLA Modules:
  0.0 1093.9 jit_solution(16823321383816352923)
XLA Ops:
  7.2 0.0 copy-start
  7.2 0.0 copy-start.3
  7.2 0.0 copy-start.4
  7.2 0.0 all-gather.5.cloned.1.call-start
  7.2 0.7 all-gather.5.cloned.1.call-update
  7.9 0.0 all-gather.3.cloned.1.call-start
  8.0 0.7 all-gather.3.cloned.1.call-update
  8.7 0.0 all-reduce.3.cloned.1.call-start
  8.8 0.0 copy-done
  8.8 0.3 fusion.19
  9.1 1.1 fusion.20
  10.2 1.1 fusion.21
  11.3 1.6 fusion.15
  12.9 0.0 copy-done.3
  12.9 0.0 copy-start.5
  12.9 0.6 fusion.13
  13.6 0.0 copy-done.4
  13.6 0.6 fusion.14
  14.2 144.2 %all-gather.5.cloned.1.call-done = bf16[1024,512]{1,0:T(8,128)(2,1)} async-done(((bf16[32,512]{1,0:T(8,128)(2,1)}), bf16[1024,512]{1,0:T(8,128)(2,1)}) %all-gather.5.cloned.1.call-update) | async-done | bytes 1048592 | tf_op jit(solution)/shard_map/all_gather | solution.py:54
  158.4 2.9 fusion.12
  161.3 0.0 copy-done.5
  161.3 137.5 %all-gather.3.cloned.1.call-done = bf16[1024,512]{1,0:T(8,128)(2,1)} async-done(((bf16[32,512]{1,0:T(8,128)(2,1)}), bf16[1024,512]{1,0:T(8,128)(2,1)}) %all-gather.3.cloned.1.call-update) | async-done | bytes 1048592 | tf_op jit(solution)/shard_map/all_gather | solution.py:53
  298.8 3.8 convert_bitcast_fusion
  302.6 0.0 all-reduce.3.cloned.1.call-update
  302.7 0.0 reduce-scatter.2.cloned.1.call-start
  302.7 133.1 %all-reduce.3.cloned.1.call-done = (bf16[1024,1024]{0,1:T(8,128)(2,1)}, bf16[1024,512]{0,1:T(8,128)(2,1)}) async-done(((bf16[1024,1024]{0,1:T(8,128)(2,1)}, bf16[1024,512]{0,1:T(8,128)(2,1)}), (bf16[1024,1024]{0,1:T(8,128)(2,1)}, bf16[1024,512]{0,1:T(8,128)(2,1)})) %all-reduce.3.cloned.1.call-update) | async-done | bytes 3145744 | tf_op jit(solution)/shard_map/psum | solution.py:58
  435.8 0.0 copy-start.1
  435.8 2.1 convert_element_type.60
  437.9 0.0 copy-done.1
  438.0 0.0 copy-start.6
  438.0 2.4 fusion.2
  440.4 0.0 copy-done.6
  440.4 0.0 copy-start.2
  440.4 1.7 convolution_convert_fusion.1
  442.1 0.0 reduce-scatter.2.cloned.1.call-update
  442.2 0.0 copy-done.2
  442.2 2.5 fusion.9
  444.6 0.2 fusion.36
  444.8 1.3 copy.13
  446.1 0.0 copy-start.7
  446.1 1.3 copy.12
  447.4 0.0 copy-done.7
  447.4 1.7 fusion.37
  449.1 638.2 %reduce-scatter.2.cloned.1.call-done = bf16[32,512]{1,0:T(8,128)(2,1)} async-done(((bf16[1024,512]{1,0:T(8,128)(2,1)}), bf16[32,512]{1,0:T(8,128)(2,1)}) %reduce-scatter.2.cloned.1.call-update) | async-done | bytes 32784 | tf_op jit(solution)/shard_map/reduce_scatter | solution.py:65
  (2 shorter events, 0.0 us)
Async XLA Ops:
  7.2 1.6 copy-start
  7.2 5.7 copy-start.3
  7.2 6.4 copy-start.4
  7.2 151.2 %all-gather.5.cloned.1.call-start = ((), (), s32[]{:S(2)}) async-start(), calls=%async_computation.3 | async-start | bytes 1081344 | tf_op jit(solution)/shard_map/all_gather | solution.py:54
  7.9 290.8 %all-gather.3.cloned.1.call-start = ((), (), s32[]{:S(2)}) async-start(), calls=%async_computation.1 | async-start | bytes 1081344 | tf_op jit(solution)/shard_map/all_gather | solution.py:53
  8.7 427.1 %all-reduce.3.cloned.1.call-start = ((), (), s32[]{:S(2)}) async-start(), calls=%async_computation.4 | async-start | bytes 6291456 | tf_op jit(solution)/shard_map/psum | solution.py:58
  12.9 148.4 %copy-start.5 = (bf16[512,512]{1,0:T(8,128)(2,1)}, bf16[512,512]{1,0:T(8,128)(2,1)S(1)}, u32[]{:S(2)}) copy-start(bf16[512,512]{1,0:T(8,128)(2,1)S(1)} %fusion.15) | copy-start | bytes 1572868
  302.7 784.7 %reduce-scatter.2.cloned.1.call-start = ((), (), s32[]{:S(2)}) async-start(), calls=%async_computation.2 | async-start | bytes 1081344 | tf_op jit(solution)/shard_map/reduce_scatter | solution.py:65
  435.8 2.1 copy-start.1
  438.0 2.4 copy-start.6
  440.4 1.8 copy-start.2
  446.1 1.3 copy-start.7
Sparse Core Ops, SparseCore 0:
  11.1 147.1 all-gather.4
  161.5 137.2 all-gather.2
  302.8 132.9 all-reduce.2
  442.3 645.0 reduce-scatter.1
where the time goes:
time: 1090 us
  waiting for transfers between devices  1050 us (96%)
  matrix products  18 us (2%)
  between operations  13.9 us (1%)
    reduce_scatter x1, waiting for transfers between devices, on_device(): lax.psum_scatter(jnp.dot(picked, w_down, preferred_element_type=jnp.float...  638 us
    all_gather x1, waiting for transfers between devices, on_device(): lax.all_gather(cotangent, 'tp', axis=0, tiled=True)  144 us
    all_gather x1, waiting for transfers between devices, on_device(): lax.all_gather(tokens, 'tp', axis=0, tiled=True)  137 us
    psum x1, waiting for transfers between devices, on_device(): lax.psum(jnp.dot(picked, w_pair, preferred_element_type=jnp.float32).asty...  133 us
  transfers between devices with their start and end apart: 4, of which 4 were waited for; matrix products, arithmetic and copies ran while one was open for 1% of the time, Pallas kernels for 0%

commit v1 on v0

v1 whole, which is shorter than its diff:
```python
import jax
import jax.numpy as jnp
from jax import lax
from jax.experimental import pallas as pl
from jax.experimental.pallas import tpu as pltpu
from jax.sharding import Mesh, PartitionSpec as P

BLOCK = 128
F32 = jnp.float32
BF16 = jnp.bfloat16

SEQ = ("xl", "y", "core")
PLANE = ("xl", "y")
Z = ("zh", "zl")
TP = ("xh", "zh", "zl")
SIZES = (2, 4, 2, 2, 4, 4)


def dequantize(codes, scales, row_place, col_place):
    rows, cols = codes.shape
    up, across = rows // BLOCK, cols // BLOCK
    picked = lax.dynamic_slice(scales, (row_place * up, col_place * across), (up, across))
    factors = jnp.broadcast_to(picked[:, None, :, None], (up, BLOCK, across, BLOCK))
    return (codes.astype(F32) * factors.reshape(rows, cols)).astype(BF16)


def shift(x, axes, size, by):
    return lax.ppermute(x, axes, [(i, (i + by) % size) for i in range(size)])


def other_core(x):
    return shift(x, "core", 2, 1)


def other_xh(x):
    return shift(x, "xh", 2, 1)


def pick(x, place):
    return lax.dynamic_index_in_dim(x, place, 0, keepdims=False)


def dot(a, b):
    return jnp.dot(a, b, preferred_element_type=F32)


def dot_nt(a, b):
    return lax.dot_general(a, b, (((1,), (1,)), ((), ())), preferred_element_type=F32)


def dot_tn(a, b):
    return lax.dot_general(a, b, (((0,), (0,)), ((), ())), preferred_element_type=F32)


def summed(x, axes):
    return lax.all_to_all(x, axes, 0, 0, tiled=False).astype(F32).sum(0)


def spread(x, count):
    copies = jnp.broadcast_to(x[None], (count,) + x.shape)
    return lax.all_to_all(copies, PLANE, 0, 0, tiled=False)


def forward_kernel(frames, near, far, near_other, far_other, out):
    width, units = near.shape[1], near.shape[2]
    own, swap = frames[:, :width], frames[:, width:]
    out[:, :units] = (dot(own, near[0]) + dot(swap, near_other[0])).astype(BF16)
    out[:, units:] = (dot(own, far[0]) + dot(swap, far_other[0])).astype(BF16)


def back_kernel(frames, near, far, near_other, far_other, out):
    width, units = near.shape[2], near.shape[1]
    own, swap = frames[:, :width], frames[:, width:]
    out[:, :units] = (dot_nt(own, near[0]) + dot_nt(swap, near_other[0])).astype(BF16)
    out[:, units:] = (dot_nt(own, far[0]) + dot_nt(swap, far_other[0])).astype(BF16)


def parts_call(kernel, name, first, count, frames, weights):
    _, width, units = weights[0].shape
    rows = frames.shape[0]
    weight = pl.BlockSpec((1, width, units), lambda k: (k + first, 0, 0))
    return pl.pallas_call(
        kernel,
        grid=(count,),
        in_specs=[pl.BlockSpec(frames.shape, lambda k: (0, 0))] + [weight] * 4,
        out_specs=pl.BlockSpec((rows, 2 * units), lambda k: (0, k)),
        out_shape=jax.ShapeDtypeStruct((rows, 2 * units * count), BF16),
        compiler_params=pltpu.CompilerParams(vmem_limit_bytes=32 * 1024 * 1024),
        cost_estimate=pl.CostEstimate(
            flops=count * 8 * rows * width * units,
            bytes_accessed=count * (8 * width * units + 4 * rows * units) + 4 * rows * width,
            transcendentals=0,
        ),
        name=name,
    )(frames, *weights)


def forward_parts(frames, weights):
    return parts_call(forward_kernel, "forward_parts", 0, 2, frames, weights)


def back_parts(frames, weights):
    return parts_call(back_kernel, "back_parts", 2, 1, frames, weights)


def on_device(
    tokens, cotangent, gate_codes, gate_scales, up_codes, up_scales, down_codes, down_scales
):
    seq_place = lax.axis_index(SEQ)
    tp_place = lax.axis_index(TP)
    core = lax.axis_index("core")
    rows, width = tokens.shape
    units = gate_codes.shape[1]
    half = rows // 2
    quarter = 16 * half

    w_near = jnp.stack(
        [
            dequantize(gate_codes, gate_scales, seq_place, tp_place),
            dequantize(up_codes, up_scales, seq_place, tp_place),
            dequantize(down_codes, down_scales, tp_place, seq_place),
        ]
    )
    w_near, tokens, cotangent = lax.optimization_barrier((w_near, tokens, cotangent))
    w_far = other_xh(w_near)
    w_near_other = other_core(w_near)

    halves = jnp.stack([tokens.reshape(2, half, width), cotangent.reshape(2, half, width)], axis=1)
    kept, got = pick(halves, core), other_core(pick(halves, 1 - core))
    mine = jnp.concatenate([kept, got], axis=2)
    frames = lax.all_gather(mine[0], Z, axis=0, tiled=True)
    w_far, frames = lax.optimization_barrier((w_far, frames))
    w_far_other = other_core(w_far)
    weights = (w_near, w_far, w_near_other, w_far_other)

    parts = forward_parts(frames, weights)
    parts, grads_mine = lax.optimization_barrier((parts, mine[1]))
    totals = summed(parts.reshape(8, rows, 4 * units), PLANE)
    grads_in = lax.all_gather(grads_mine, Z, axis=0, tiled=True)
    gate_sum = totals[:, : 2 * units]
    up_sum = totals[:, 2 * units :]
    sigma = jax.nn.sigmoid(gate_sum)
    silu = gate_sum * sigma
    hidden = (silu * up_sum).astype(BF16)

    back = back_parts(grads_in, weights)
    frames, back, grads_in = lax.optimization_barrier((frames, back, grads_in))
    both = jnp.concatenate(
        [jnp.broadcast_to(hidden[None], (8, rows, 2 * units)), back.reshape(8, rows, 2 * units)], axis=2
    )
    both = lax.all_to_all(both, PLANE, 0, 0, tiled=False)
    hidden_grad = both[:, :, 2 * units :].astype(F32).sum(0)
    gate_grad = (hidden_grad * up_sum * sigma * (1.0 + gate_sum * (1.0 - sigma))).astype(BF16)
    up_grad = (hidden_grad * silu).astype(BF16)

    hidden_own = both[:, :, : 2 * units].reshape(quarter, 2 * units)
    hidden_other = other_core(hidden_own)
    w_down_pair = jnp.concatenate([w_near[2], w_far[2]])
    mixed = jnp.stack(
        [dot(hidden_own, w_down_pair).astype(BF16), dot(hidden_other, w_down_pair).astype(BF16)]
    )
    mixed = mixed.reshape(2, 16, half, width).transpose(1, 0, 2, 3)

    kept = jnp.concatenate([gate_grad[:, :units], up_grad[:, :units]], axis=1)
    sent = jnp.concatenate([gate_grad[:, units:], up_grad[:, units:]], axis=1)
    grads_own = spread(jnp.stack([kept, other_xh(sent)]), 8).reshape(8, 2, rows, 2 * units)

    swap = other_core(jnp.concatenate([frames[:, width:], grads_in[:, width:]], axis=1))
    near = jnp.concatenate([frames[:, :width], grads_in[:, :width]], axis=1)
    near, swap = lax.optimization_barrier((near, swap))
    far = other_xh(jnp.concatenate([near, swap]))
    units_far = other_xh(jnp.concatenate([hidden_own[:, units:], hidden_other[:, units:]]))

    grads_own, mixed = lax.optimization_barrier((grads_own, mixed))
    grads_other = other_core(grads_own)
    mixed = summed(mixed, Z)
    mixed = jnp.where(core == 0, mixed, mixed[::-1]).astype(BF16).reshape(rows, width)
    mixed, far, units_far = lax.optimization_barrier((mixed, far, units_far))

    def over_frames(near, swap, far, near_right, swap_right, far_right):
        return dot_tn(near, near_right) + dot_tn(swap, swap_right) + dot_tn(far, far_right)

    flat = lambda x, place, part: x[:, place].reshape(quarter, 2 * units)[:, part]

    def pair_grad(part):
        return over_frames(
            near[:, :width],
            swap[:, :width],
            far[:, :width],
            flat(grads_own, 0, part),
            flat(grads_other, 0, part),
            jnp.concatenate([flat(grads_own, 1, part), flat(grads_other, 1, part)]),
        )

    grad_gate, grad_up = pair_grad(slice(0, units)), pair_grad(slice(units, 2 * units))
    grad_down = over_frames(
        hidden_own[:, :units],
        hidden_other[:, :units],
        units_far,
        near[:, width:],
        swap[:, width:],
        far[:, width:],
    )
    return (mixed, grad_gate, grad_up, grad_down)


def solution(mesh):
    named = Mesh(mesh.devices.reshape(SIZES), SEQ + TP)
    return jax.shard_map(
        on_device,
        mesh=named,
        in_specs=(
            P(TP, SEQ),
            P(TP, SEQ),
            P(SEQ, TP),
            P(),
            P(SEQ, TP),
            P(),
            P(TP, SEQ),
            P(),
        ),
        out_specs=(P(TP, SEQ), P(SEQ, TP), P(SEQ, TP), P(TP, SEQ)),
        check_vma=False,
    )
```

time: 1090 us -> 203 us (0.19)
  waiting for transfers between devices: 1050 us -> 33.7 us
  blocking collectives: 0 us -> 69.7 us
  starting transfers between devices: 0.16 us -> 50.9 us
  local copies, waits for them, and re-layouts: 2.83 us -> 17.3 us
  between operations: 13.9 us -> 1.19 us
    reduce_scatter x1 -> x0, waiting for transfers between devices: 638 us -> none  [on_device(): lax.psum_scatter(jnp.dot(picked, w_down, preferred_element_type=jnp.float...]
    all_gather x2 -> x0, waiting for transfers between devices: 282 us -> none  [the longest x1 144 us: on_device(): lax.all_gather(cotangent, 'tp', axis=0, tiled=True)]
    psum x1 -> x0, waiting for transfers between devices: 133 us -> none  [on_device(): lax.psum(jnp.dot(picked, w_pair, preferred_element_type=jnp.float32).asty...]
    all_gather x0 -> x2, blocking collectives: none -> 69.7 us  [the longest x1 38.3 us: on_device(): frames = lax.all_gather(mine[0], Z, axis=0, tiled=True)]
    all_to_all x0 -> x4, waiting for transfers between devices: none -> 30.2 us  [the longest x2 24.8 us: summed(): return lax.all_to_all(x, axes, 0, 0, tiled=False).astype(F32).sum(0)]
    ppermute x0 -> x10, starting transfers between devices: none -> 28.8 us  [shift(): return lax.ppermute(x, axes, [(i, (i + by) % size) for i in range(size)])]
    all_to_all x0 -> x4, starting transfers between devices: none -> 22.1 us  [the longest x2 11.7 us: summed(): return lax.all_to_all(x, axes, 0, 0, tiled=False).astype(F32).sum(0)]
  transfers between devices with their start and end apart: 4 -> 14, of which waited for: 4 -> 4; matrix products, arithmetic and copies ran while one was open for 1% -> 11% of each run, Pallas kernels for 0% -> 0%
where the time goes in v1:
time: 203 us; the launch traced here: 200 us
  blocking collectives  69.7 us (34%)
  starting transfers between devices  50.9 us (25%)
  waiting for transfers between devices  33.7 us (17%)
  local copies, waits for them, and re-layouts  17.3 us (9%)
  matrix products  14.4 us (7%)
  other arithmetic  11 us (5%)
  Pallas kernels  2.21 us (1%)
    all_gather x1, blocking collectives, on_device(): frames = lax.all_gather(mine[0], Z, axis=0, tiled=True)  38.3 us
    all_gather x1, blocking collectives, on_device(): grads_in = lax.all_gather(grads_mine, Z, axis=0, tiled=True)  31.3 us
    ppermute x10, starting transfers between devices, shift(): return lax.ppermute(x, axes, [(i, (i + by) % size) for i in range(size)])  28.8 us
    all_to_all x2, waiting for transfers between devices, summed(): return lax.all_to_all(x, axes, 0, 0, tiled=False).astype(F32).sum(0)  24.8 us
    dot_general x9, matrix products, dot_tn(): lax.dot_general(a, b, (((0,), (0,)), ((), ())), preferred_element_type=F32)  12.5 us
    all_to_all x2, starting transfers between devices, summed(): return lax.all_to_all(x, axes, 0, 0, tiled=False).astype(F32).sum(0)  11.7 us
    unnamed x38, local copies, waits for them, and re-layouts  6.19 us
    all_to_all x1, starting transfers between devices, on_device(): both = lax.all_to_all(both, PLANE, 0, 0, tiled=False)  5.44 us
  transfers between devices with their start and end apart: 14, of which 4 were waited for; matrix products, arithmetic and copies ran while one was open for 11% of the time, Pallas kernels for 0%

profile of v1, /device:TPU:24, one launch (start us, length us, event | category | flops | bytes accessed | tf_op | source)
XLA Modules:
  0.0 200.4 jit_solution(7973408436965657091)
XLA Ops:
  0.6 0.8 dynamic_slice.18
  1.5 0.8 dynamic_slice.16
  2.3 0.8 dynamic_slice.17
  3.0 0.2 broadcast_in_dim.12
  3.2 1.2 fusion.5
  4.5 0.2 broadcast_in_dim.10
  4.7 0.2 broadcast_in_dim.11
  4.9 0.6 copy-done.15
  5.7 0.4 fusion.3
  6.3 4.9 %collective-permute-start = (bf16[3,512,512]{2,1,0:T(8,128)(2,1)S(1)}, bf16[3,512,512]{2,1,0:T(8,128)(2,1)S(1)}, u32[]{:S(2)}, u32[]{:S(2)}) collective-permute-start(bf16[3,512,512]{2,1,0:T(8,128)(2,1)S(1)} %pad_maximum_fusion.near), channel_id=1, source_target_pairs={{0,16},{16,0},{1,17},{17,1},{2,18},{18,2},{3,19},{19,3},{4,20},{20... | collective-permute-start | bytes 4718600 | tf_op jit(solution)/shard_map/ppermute | solution.py:28
  11.3 1.9 collective-permute-start.1
  13.2 2.4 %collective-permute-start.2 = (bf16[3,512,512]{2,1,0:T(8,128)(2,1)S(1)}, bf16[3,512,512]{2,1,0:T(8,128)(2,1)S(1)}, u32[]{:S(2)}, u32[]{:S(2)}) collective-permute-start(bf16[3,512,512]{2,1,0:T(8,128)(2,1)S(1)} %pad_maximum_fusion.near), channel_id=1, source_target_pairs={{0,32},{32,0},{1,33},{33,1},{2,34},{34,2},{3,35},{35,3},{4,36},{36... | collective-permute-start | bytes 4718600 | tf_op jit(solution)/shard_map/ppermute | solution.py:28
  15.7 38.3 %all-gather = bf16[1,256,1024]{2,1,0:T(8,128)(2,1)S(1)} all-gather(bf16[1,16,1024]{2,1,0:T(8,128)(2,1)S(1)} %get-tuple-element.57), channel_id=2, replica_groups=mesh['xl'=2,'y'=4,'core'=2,'xh'=2,'zh'=4,'zl'=4] {'zh','zl'}, dimensions={1}, use_global_device_ids=true | all-gather | bytes 557056 | tf_op jit(solution)/shard_map/all_gather | solution.py:131
  54.0 1.9 collective-permute-start.3
  55.9 3.4 %collective-permute-done.3.far_other = bf16[3,512,512]{2,1,0:T(8,128)(2,1)S(1)} collective-permute-done((bf16[3,512,512]{2,1,0:T(8,128)(2,1)S(1)}, bf16[3,512,512]{2,1,0:T(8,128)(2,1)S(1)}, u32[]{:S(2)}, u32[]{:S(2)}) %collective-permute-start.3) | collective-permute-done | bytes 1572896 | tf_op jit(solution)/shard_map/ppermute | solution.py:28
  59.3 1.5 forward_parts.1
  60.8 1.0 copy-done.7
  61.8 4.7 %all-to-all-start = ((bf16[8,32,2048]{2,1,0:T(8,128)(2,1)}), bf16[8,32,2048]{2,1,0:T(8,128)(2,1)}, u32[]{:S(2)}, u32[]{:S(2)}) async-start(bf16[8,32,2048]{2,1,0:T(8,128)(2,1)} %bitcast.71), calls=%async_computation | async-start | bytes 2097152 | tf_op jit(solution)/shard_map/all_to_all | solution.py:56
  66.5 31.3 %all_gather.7.frames = bf16[256,1024]{1,0:T(8,128)(2,1)S(1)} all-gather(bf16[16,1024]{1,0:T(8,128)(2,1)S(1)} %get-tuple-element.27), channel_id=1, replica_groups=mesh['xl'=2,'y'=4,'core'=2,'xh'=2,'zh'=4,'zl'=4] {'zh','zl'}, dimensions={0}, use_global_device_ids=true | all-gather | bytes 557056 | tf_op jit(solution)/shard_map/all_gather | solution.py:139
  97.8 1.4 copy-done.1
  99.2 1.4 copy-done.3
  100.7 0.7 back_parts.1
  101.4 0.8 copy-done.4
  102.2 0.8 copy-done.8
  103.0 1.4 convert_reduce_fusion
  104.6 1.1 pad_maximum_fusion.1
  105.6 5.4 %all-to-all-start.1 = ((bf16[8,32,2048]{2,1,0:T(8,128)(2,1)}), bf16[8,32,2048]{2,1,0:T(8,128)(2,1)}, u32[]{:S(2)}, u32[]{:S(2)}) async-start(bf16[8,32,2048]{2,1,0:T(8,128)(2,1)} %pad_maximum_fusion.1), calls=%async_computation.1 | async-start | bytes 2097152 | tf_op jit(solution)/shard_map/all_to_all | solution.py:151
  111.1 0.8 slice_bitcast_fusion.1
  111.9 0.8 slice_bitcast_fusion
  112.7 1.1 fusion.47
  113.8 0.9 pad_maximum_fusion.7
  114.7 1.9 collective-permute-start.6
  116.6 3.8 %all-to-all-done.1 = bf16[8,32,2048]{2,1,0:T(8,128)(2,1)} async-done(((bf16[8,32,2048]{2,1,0:T(8,128)(2,1)}), bf16[8,32,2048]{2,1,0:T(8,128)(2,1)}, u32[]{:S(2)}, u32[]{:S(2)}) %all-to-all-start.1) | async-done | bytes 1048608 | tf_op jit(solution)/shard_map/all_to_all | solution.py:151
  120.4 1.1 convert_reduce_fusion.2
  121.7 4.6 %collective-permute-start.4 = (bf16[32,1024]{1,0:T(8,128)(2,1)S(1)}, bf16[32,1024]{1,0:T(8,128)(2,1)S(1)}, u32[]{:S(2)}, u32[]{:S(2)}) collective-permute-start(bf16[32,1024]{1,0:T(8,128)(2,1)S(1)} %pad_maximum_fusion.10), channel_id=1, source_target_pairs={{0,16},{16,0},{1,17},{17,1},{2,18},{18,2},{3,19},{19,3},{4,20},{20... | collective-permute-start | bytes 196616 | tf_op jit(solution)/shard_map/ppermute | solution.py:28
  126.3 1.1 slice.168
  127.4 1.9 collective-permute-start.5
  129.4 1.1 broadcast_in_dim.14
  130.5 5.0 %all-to-all-start.2 = ((bf16[8,2,32,1024]{3,2,1,0:T(8,128)(2,1)}), bf16[8,2,32,1024]{3,2,1,0:T(8,128)(2,1)S(1)}, u32[]{:S(2)}, u32[]{:S(2)}) async-start(bf16[8,2,32,1024]{3,2,1,0:T(8,128)(2,1)} %broadcast_in_dim.14), calls=%async_computation.2 | async-start | bytes 2097152 | tf_op jit(solution)/shard_map/all_to_all | solution.py:61
  135.5 1.0 pad_maximum_fusion.3
  136.6 4.6 %collective-permute-start.7 = (bf16[512,1024]{1,0:T(8,128)(2,1)}, bf16[512,1024]{1,0:T(8,128)(2,1)}, u32[]{:S(2)}, u32[]{:S(2)}) collective-permute-start(bf16[512,1024]{1,0:T(8,128)(2,1)} %pad_maximum_fusion.3), channel_id=1, source_target_pairs={{0,16},{16,0},{1,17},{17,1},{2,18},{18,2},{3,19},{19,3},{4,20},{20... | collective-permute-start | bytes 3145736 | tf_op jit(solution)/shard_map/ppermute | solution.py:28
  141.2 0.4 convolution_convert_fusion.1
  141.7 1.0 slice.170
  142.6 0.8 pad_maximum_fusion.8
  143.5 2.8 %collective-permute-start.8 = (bf16[512,512]{1,0:T(8,128)(2,1)}, bf16[512,512]{1,0:T(8,128)(2,1)}, u32[]{:S(2)}, u32[]{:S(2)}) collective-permute-start(bf16[512,512]{1,0:T(8,128)(2,1)} %pad_maximum_fusion.8), channel_id=1, source_target_pairs={{0,16},{16,0},{1,17},{17,1},{2,18},{18,2},{3,19},{19,3},{4,20},{20... | collective-permute-start | bytes 1572872 | tf_op jit(solution)/shard_map/ppermute | solution.py:28
  146.3 1.5 convolution_convert_fusion
  147.8 0.8 maximum_bitcast_fusion
  148.6 1.7 all-to-all-done.2
  150.3 1.9 collective-permute-start.9
  152.2 1.3 fusion.15
  153.4 1.3 convolution_add_fusion.3
  154.7 7.0 %all-to-all-start.3 = ((bf16[16,2,16,512]{3,2,1,0:T(8,128)(2,1)}), bf16[16,2,16,512]{3,2,1,0:T(8,128)(2,1)}, u32[]{:S(2)}, u32[]{:S(2)}) async-start(bf16[16,2,16,512]{3,2,1,0:T(8,128)(2,1)} %maximum_bitcast_fusion), calls=%async_computation.3 | async-start | bytes 1048576 | tf_op jit(solution)/shard_map/all_to_all | solution.py:56
  161.8 0.7 fusion.44
  162.5 1.3 fusion.43
  163.8 0.3 fusion.21
  164.2 1.3 convolution_add_fusion.5
  165.5 0.3 fusion.18
  165.8 0.3 convolution_add_fusion.4
  166.2 24.8 %all-to-all-done.3 = bf16[16,2,16,512]{3,2,1,0:T(8,128)(2,1)} async-done(((bf16[16,2,16,512]{3,2,1,0:T(8,128)(2,1)}), bf16[16,2,16,512]{3,2,1,0:T(8,128)(2,1)}, u32[]{:S(2)}, u32[]{:S(2)}) %all-to-all-start.3) | async-done | bytes 524320 | tf_op jit(solution)/shard_map/all_to_all | solution.py:56
  190.9 1.1 convert_reduce_fusion.1
  192.1 0.6 fusion.31
  192.7 2.7 %convolution_add_fusion = f32[512,512]{1,0:T(8,128)} fusion(f32[512,512]{1,0:T(8,128)S(1)} %convolution_add_fusion.3, bf16[512,512]{1,0:T(8,128)(2,1)} %collective-permute-done.8, bf16[512,1024]{1,0:T(8,128)(2,1)} %collective-permute-done.7), kind=kOutput, calls=%fused_computation.2 | convolution fusion | flops 268697600 | bytes 3145728 | tf_op jit(solution)/shard_map/dot_general | solution.py:52
  195.5 2.5 %convolution_add_fusion.2 = f32[512,512]{1,0:T(8,128)} fusion(f32[512,512]{1,0:T(8,128)S(1)} %copy-done.10, bf16[256,512]{1,0:T(8,128)(2,1)S(1)} %get-tuple-element.45, bf16[256,512]{1,0:T(8,128)(2,1)S(1)} %copy-done.12, bf16[512,1024]{1,0:T(8,128)(2,1)} %collective-permute-done.7), kind=kOutput, calls=%fused_computation.4 | convolution fusion | flops 269746176 | bytes 3145728 | tf_op jit(solution)/shard_map/dot_general | solution.py:52
  197.9 2.5 %convolution_add_fusion.1 = f32[512,512]{1,0:T(8,128)} fusion(f32[512,512]{1,0:T(8,128)S(1)} %convolution_add_fusion.4, bf16[256,512]{1,0:T(8,128)(2,1)S(1)} %get-tuple-element.44, bf16[256,512]{1,0:T(8,128)(2,1)S(1)} %get-tuple-element.42, bf16[512,1024]{1,0:T(8,128)(2,1)} %collective-permute-done.7), kind=kOutput, calls=%fused_computation.3 | convolution fusion | flops 269746176 | bytes 3145728 | tf_op jit(solution)/shard_map/dot_general | solution.py:52
  (59 shorter events, 1.0 us)
Async XLA Ops:
  4.5 1.0 copy-start.15
  4.5 1.2 copy-start.16
  6.1 5.2 %copy-start.17 = (bf16[32,512]{1,0:T(8,128)(2,1)S(1)}, bf16[32,512]{1,0:T(8,128)(2,1)}, u32[]{:S(2)}) copy-start(bf16[32,512]{1,0:T(8,128)(2,1)} %param.8) | copy-start | bytes 98308
  6.1 5.2 %copy-start.18 = (bf16[32,512]{1,0:T(8,128)(2,1)S(1)}, bf16[32,512]{1,0:T(8,128)(2,1)}, u32[]{:S(2)}) copy-start(bf16[32,512]{1,0:T(8,128)(2,1)} %param.9) | copy-start | bytes 98308
  6.3 47.7 %collective-permute-start = (bf16[3,512,512]{2,1,0:T(8,128)(2,1)S(1)}, bf16[3,512,512]{2,1,0:T(8,128)(2,1)S(1)}, u32[]{:S(2)}, u32[]{:S(2)}) collective-permute-start(bf16[3,512,512]{2,1,0:T(8,128)(2,1)S(1)} %pad_maximum_fusion.near), channel_id=1, source_target_pairs={{0,16},{16,0},{1,17},{17,1},{2,18},{18,2},{3,19},{19,3},{4,20},{20... | collective-permute-start | bytes 4718600 | tf_op jit(solution)/shard_map/ppermute | solution.py:28
  11.3 4.3 %collective-permute-start.1 = (bf16[2,16,512]{2,1,0:T(8,128)(2,1)S(1)}, bf16[2,16,512]{2,1,0:T(8,128)(2,1)S(1)}, u32[]{:S(2)}, u32[]{:S(2)}) collective-permute-start(bf16[2,16,512]{2,1,0:T(8,128)(2,1)S(1)} %get-tuple-element.58), channel_id=1, source_target_pairs={{0,32},{32,0},{1,33},{33,1},{2,34},{34,2},{3,35},{35,3},{4,36},{36... | collective-permute-start | bytes 98312 | tf_op jit(solution)/shard_map/ppermute | solution.py:28
  13.2 42.7 %collective-permute-start.2 = (bf16[3,512,512]{2,1,0:T(8,128)(2,1)S(1)}, bf16[3,512,512]{2,1,0:T(8,128)(2,1)S(1)}, u32[]{:S(2)}, u32[]{:S(2)}) collective-permute-start(bf16[3,512,512]{2,1,0:T(8,128)(2,1)S(1)} %pad_maximum_fusion.near), channel_id=1, source_target_pairs={{0,32},{32,0},{1,33},{33,1},{2,34},{34,2},{3,35},{35,3},{4,36},{36... | collective-permute-start | bytes 4718600 | tf_op jit(solution)/shard_map/ppermute | solution.py:28
  54.0 6.8 %copy-start.5 = (bf16[1,256,1024]{2,1,0:T(8,128)(2,1)}, bf16[1,256,1024]{2,1,0:T(8,128)(2,1)S(1)}, u32[]{:S(2)}) copy-start(bf16[1,256,1024]{2,1,0:T(8,128)(2,1)S(1)} %all-gather) | copy-start | bytes 1572868
  54.0 5.3 %collective-permute-start.3 = (bf16[3,512,512]{2,1,0:T(8,128)(2,1)S(1)}, bf16[3,512,512]{2,1,0:T(8,128)(2,1)S(1)}, u32[]{:S(2)}, u32[]{:S(2)}) collective-permute-start(bf16[3,512,512]{2,1,0:T(8,128)(2,1)S(1)} %collective-permute-done.far), channel_id=1, source_target_pairs={{0,32},{32,0},{1,33},{33,1},{2,34},{34,2},{3,35},{35,3},{4,36},{36... | collective-permute-start | bytes 4718600 | tf_op jit(solution)/shard_map/ppermute | solution.py:28
  55.9 4.9 %copy-start = (bf16[3,512,512]{2,1,0:T(8,128)(2,1)}, bf16[3,512,512]{2,1,0:T(8,128)(2,1)S(1)}, u32[]{:S(2)}) copy-start(bf16[3,512,512]{2,1,0:T(8,128)(2,1)S(1)} %collective-permute-done.2.near_other) | copy-start | bytes 4718596
  59.3 1.5 copy-start.2
  60.8 1.0 copy-start.7
  61.8 41.2 %all-to-all-start = ((bf16[8,32,2048]{2,1,0:T(8,128)(2,1)}), bf16[8,32,2048]{2,1,0:T(8,128)(2,1)}, u32[]{:S(2)}, u32[]{:S(2)}) async-start(bf16[8,32,2048]{2,1,0:T(8,128)(2,1)} %bitcast.71), calls=%async_computation | async-start | bytes 2097152 | tf_op jit(solution)/shard_map/all_to_all | solution.py:56
  97.8 1.4 copy-start.1
  99.2 1.4 copy-start.3
  101.4 0.8 copy-start.4
  102.2 0.8 copy-start.8
  103.0 1.6 copy-start.9
  105.6 14.8 %all-to-all-start.1 = ((bf16[8,32,2048]{2,1,0:T(8,128)(2,1)}), bf16[8,32,2048]{2,1,0:T(8,128)(2,1)}, u32[]{:S(2)}, u32[]{:S(2)}) async-start(bf16[8,32,2048]{2,1,0:T(8,128)(2,1)} %pad_maximum_fusion.1), calls=%async_computation.1 | async-start | bytes 2097152 | tf_op jit(solution)/shard_map/all_to_all | solution.py:151
  111.9 1.9 copy-start.6
  114.7 20.8 %collective-permute-start.6 = (bf16[256,1024]{1,0:T(8,128)(2,1)}, bf16[256,1024]{1,0:T(8,128)(2,1)S(1)}, u32[]{:S(2)}, u32[]{:S(2)}) collective-permute-start(bf16[256,1024]{1,0:T(8,128)(2,1)} %pad_maximum_fusion.7), channel_id=1, source_target_pairs={{0,32},{32,0},{1,33},{33,1},{2,34},{34,2},{3,35},{35,3},{4,36},{36... | collective-permute-start | bytes 1572872 | tf_op jit(solution)/shard_map/ppermute | solution.py:28
  121.7 7.7 %collective-permute-start.4 = (bf16[32,1024]{1,0:T(8,128)(2,1)S(1)}, bf16[32,1024]{1,0:T(8,128)(2,1)S(1)}, u32[]{:S(2)}, u32[]{:S(2)}) collective-permute-start(bf16[32,1024]{1,0:T(8,128)(2,1)S(1)} %pad_maximum_fusion.10), channel_id=1, source_target_pairs={{0,16},{16,0},{1,17},{17,1},{2,18},{18,2},{3,19},{19,3},{4,20},{20... | collective-permute-start | bytes 196616 | tf_op jit(solution)/shard_map/ppermute | solution.py:28
  127.4 13.8 %copy-start.11 = (bf16[8,32,1024]{2,1,0:T(8,128)(2,1)}, bf16[8,32,1024]{2,1,0:T(8,128)(2,1)S(1)}, u32[]{:S(2)}) copy-start(bf16[8,32,1024]{2,1,0:T(8,128)(2,1)S(1)} %slice.168) | copy-start | bytes 1572868
  127.4 14.3 %collective-permute-start.5 = (bf16[256,1024]{1,0:T(8,128)(2,1)S(1)}, bf16[256,1024]{1,0:T(8,128)(2,1)}, u32[]{:S(2)}, u32[]{:S(2)}) collective-permute-start(bf16[256,1024]{1,0:T(8,128)(2,1)S(1)} %bitcast.76), channel_id=1, source_target_pairs={{0,32},{32,0},{1,33},{33,1},{2,34},{34,2},{3,35},{35,3},{4,36},{36... | collective-permute-start | bytes 1572872 | tf_op jit(solution)/shard_map/ppermute | solution.py:28
  130.5 19.8 %all-to-all-start.2 = ((bf16[8,2,32,1024]{3,2,1,0:T(8,128)(2,1)}), bf16[8,2,32,1024]{3,2,1,0:T(8,128)(2,1)S(1)}, u32[]{:S(2)}, u32[]{:S(2)}) async-start(bf16[8,2,32,1024]{3,2,1,0:T(8,128)(2,1)} %broadcast_in_dim.14), calls=%async_computation.2 | async-start | bytes 2097152 | tf_op jit(solution)/shard_map/all_to_all | solution.py:61
  135.5 5.7 %copy-start.13 = (bf16[512,512]{1,0:T(8,128)(2,1)S(1)}, bf16[512,512]{1,0:T(8,128)(2,1)}, u32[]{:S(2)}) copy-start(bf16[512,512]{1,0:T(8,128)(2,1)} %slice_bitcast_fusion.1) | copy-start | bytes 1572868
  135.5 5.7 %copy-start.14 = (bf16[512,512]{1,0:T(8,128)(2,1)S(1)}, bf16[512,512]{1,0:T(8,128)(2,1)}, u32[]{:S(2)}) copy-start(bf16[512,512]{1,0:T(8,128)(2,1)} %slice_bitcast_fusion) | copy-start | bytes 1572868
  136.6 56.1 %collective-permute-start.7 = (bf16[512,1024]{1,0:T(8,128)(2,1)}, bf16[512,1024]{1,0:T(8,128)(2,1)}, u32[]{:S(2)}, u32[]{:S(2)}) collective-permute-start(bf16[512,1024]{1,0:T(8,128)(2,1)} %pad_maximum_fusion.3), channel_id=1, source_target_pairs={{0,16},{16,0},{1,17},{17,1},{2,18},{18,2},{3,19},{19,3},{4,20},{20... | collective-permute-start | bytes 3145736 | tf_op jit(solution)/shard_map/ppermute | solution.py:28
  143.5 49.2 %collective-permute-start.8 = (bf16[512,512]{1,0:T(8,128)(2,1)}, bf16[512,512]{1,0:T(8,128)(2,1)}, u32[]{:S(2)}, u32[]{:S(2)}) collective-permute-start(bf16[512,512]{1,0:T(8,128)(2,1)} %pad_maximum_fusion.8), channel_id=1, source_target_pairs={{0,16},{16,0},{1,17},{17,1},{2,18},{18,2},{3,19},{19,3},{4,20},{20... | collective-permute-start | bytes 1572872 | tf_op jit(solution)/shard_map/ppermute | solution.py:28
  150.3 12.3 %collective-permute-start.9 = (bf16[8,2,32,1024]{3,2,1,0:T(8,128)(2,1)S(1)}, bf16[8,2,32,1024]{3,2,1,0:T(8,128)(2,1)}, u32[]{:S(2)}, u32[]{:S(2)}) collective-permute-start(bf16[8,2,32,1024]{3,2,1,0:T(8,128)(2,1)S(1)} %all-to-all-done.2), channel_id=1, source_target_pairs={{0,32},{32,0},{1,33},{33,1},{2,34},{34,2},{3,35},{35,3},{4,36},{36... | collective-permute-start | bytes 3145736 | tf_op jit(solution)/shard_map/ppermute | solution.py:28
  154.7 36.2 %all-to-all-start.3 = ((bf16[16,2,16,512]{3,2,1,0:T(8,128)(2,1)}), bf16[16,2,16,512]{3,2,1,0:T(8,128)(2,1)}, u32[]{:S(2)}, u32[]{:S(2)}) async-start(bf16[16,2,16,512]{3,2,1,0:T(8,128)(2,1)} %maximum_bitcast_fusion), calls=%async_computation.3 | async-start | bytes 1048576 | tf_op jit(solution)/shard_map/all_to_all | solution.py:56
  192.7 2.8 %copy-start.10 = (f32[512,512]{1,0:T(8,128)S(1)}, f32[512,512]{1,0:T(8,128)}, u32[]{:S(2)}) copy-start(f32[512,512]{1,0:T(8,128)} %convolution_add_fusion.5) | copy-start | bytes 3145732
  192.7 2.8 %copy-start.12 = (bf16[256,512]{1,0:T(8,128)(2,1)S(1)}, bf16[256,512]{1,0:T(8,128)(2,1)}, u32[]{:S(2)}) copy-start(bf16[256,512]{1,0:T(8,128)(2,1)} %get-tuple-element.43) | copy-start | bytes 786436

commit v2 on v1

v2 whole, which is shorter than its diff:
```python
import jax
import jax.numpy as jnp
from jax import lax
from jax.experimental import pallas as pl
from jax.experimental.pallas import tpu as pltpu
from jax.sharding import Mesh, PartitionSpec as P

BLOCK = 128
LANES = 128
F32 = jnp.float32
BF16 = jnp.bfloat16

SEQ = ("xl", "y", "core")
PLANE = ("xl", "y")
Z = ("zh", "zm", "zn")
TP = ("xh", "zh", "zm", "zn")
SIZES = (2, 4, 2, 2, 4, 2, 2)


def dequantize_kernel(place, gate_scales, up_scales, down_scales, gate, up, down, out):
    low, turn = place[0] % 2 == 0, (LANES - 4 * place[1]) % LANES
    for kind, (codes, scales) in enumerate(((gate, gate_scales), (up, up_scales), (down, down_scales))):
        factors = pltpu.roll(jnp.where(low, scales[:4], scales[4:]), turn, 1)
        for w in range(4):
            for u in range(4):
                r, c = (u, w) if kind == 2 else (w, u)
                rows, cols = slice(r * BLOCK, (r + 1) * BLOCK), slice(c * BLOCK, (c + 1) * BLOCK)
                factor = jnp.broadcast_to(factors[w : w + 1, u : u + 1], (BLOCK, BLOCK))
                out[kind, rows, cols] = (codes[rows, cols].astype(F32) * factor).astype(BF16)


def dequantize(place, codes, scales):
    size = codes[0].shape
    scale = pl.BlockSpec((8, LANES), lambda i, place: (place[0] // 2, 0))
    return pl.pallas_call(
        dequantize_kernel,
        grid_spec=pltpu.PrefetchScalarGridSpec(
            num_scalar_prefetch=1,
            grid=(1,),
            in_specs=[scale] * 3 + [pl.BlockSpec(size, lambda i, place: (0, 0))] * 3,
            out_specs=pl.BlockSpec((3,) + size, lambda i, place: (0, 0, 0)),
        ),
        out_shape=jax.ShapeDtypeStruct((3,) + size, BF16),
        compiler_params=pltpu.CompilerParams(vmem_limit_bytes=56 * 1024 * 1024),
        name="dequantize",
    )(place, *scales, *codes)


def shift(x, axes, size, by):
    return lax.ppermute(x, axes, [(i, (i + by) % size) for i in range(size)])


def other_core(x):
    return shift(x, "core", 2, 1)


def other_xh(x):
    return shift(x, "xh", 2, 1)


def pick(x, place):
    return lax.dynamic_index_in_dim(x, place, 0, keepdims=False)


def dot(a, b):
    return jnp.dot(a, b, preferred_element_type=F32)


def dot_nt(a, b):
    return lax.dot_general(a, b, (((1,), (1,)), ((), ())), preferred_element_type=F32)


def dot_tn(a, b):
    return lax.dot_general(a, b, (((0,), (0,)), ((), ())), preferred_element_type=F32)


def summed(x, axes):
    return lax.all_to_all(x, axes, 0, 0, tiled=False).astype(F32).sum(0)


def halved(x, place, pairs):
    x = x.reshape((x.shape[0] // 2, 2) + x.shape[1:])
    own, away = (lax.dynamic_index_in_dim(x, p, 1, keepdims=False) for p in (place, 1 - place))
    return (own.astype(F32) + lax.ppermute(away, Z, pairs).astype(F32)).astype(BF16)


def spread(x, count):
    copies = jnp.broadcast_to(x[None], (count,) + x.shape)
    return lax.all_to_all(copies, PLANE, 0, 0, tiled=False)


def forward_kernel(frames, tail, near, far, near_other, far_other, out):
    width, units = near.shape[1], near.shape[2]
    kind = pl.program_id(0)

    @pl.when(kind < 2)
    def _():
        own, swap = frames[:, :width], frames[:, width : 2 * width]
        out[:, :units] = (dot(own, near[0]) + dot(swap, near_other[0])).astype(BF16)
        out[:, units:] = (dot(own, far[0]) + dot(swap, far_other[0])).astype(BF16)

    @pl.when(kind == 2)
    def _():
        own = frames[:, 2 * width : 3 * width]
        swap = jnp.concatenate([frames[:, 3 * width :], tail[...]], axis=1)
        out[:, :units] = (dot_nt(own, near[0]) + dot_nt(swap, near_other[0])).astype(BF16)
        out[:, units:] = (dot_nt(own, far[0]) + dot_nt(swap, far_other[0])).astype(BF16)


def forward_parts(frames, tail, near, far, near_other, far_other):
    count, width, units = near.shape
    whole = lambda x: pl.BlockSpec(x.shape, lambda k: (0, 0))
    weight = pl.BlockSpec((1, width, units), lambda k: (k, 0, 0))
    return pl.pallas_call(
        forward_kernel,
        grid=(count,),
        in_specs=[whole(frames), whole(tail), weight, weight, weight, weight],
        out_specs=pl.BlockSpec((frames.shape[0], 2 * units), lambda k: (0, k)),
        out_shape=jax.ShapeDtypeStruct((frames.shape[0], 2 * units * count), BF16),
        compiler_params=pltpu.CompilerParams(vmem_limit_bytes=32 * 1024 * 1024),
        cost_estimate=pl.CostEstimate(flops=12 * frames.shape[0] * 2 * width * units, bytes_accessed=12 * width * units * 2 + 6 * frames.shape[0] * units * 2, transcendentals=0),
        name="forward_parts",
    )(frames, tail, near, far, near_other, far_other)


def plane_kernel(arrived, hidden, kept, sent):
    units = arrived.shape[2] // 6
    places = arrived.shape[0]
    total = arrived[0].astype(F32)
    for place in range(1, places):
        total = total + arrived[place].astype(F32)
    gate_sum, up_sum, hidden_grad = (total[:, 2 * k * units : 2 * (k + 1) * units] for k in range(3))
    sigma = jax.nn.sigmoid(gate_sum)
    silu = gate_sum * sigma
    out = (silu * up_sum).astype(BF16)
    for place in range(places):
        hidden[place] = out
    gate_grad = (hidden_grad * up_sum * sigma * (1.0 + gate_sum * (1.0 - sigma))).astype(BF16)
    up_grad = (hidden_grad * silu).astype(BF16)
    kept[:, :units], kept[:, units:] = gate_grad[:, :units], up_grad[:, :units]
    sent[:, :units], sent[:, units:] = gate_grad[:, units:], up_grad[:, units:]


def plane_parts(arrived):
    places, rows, columns = arrived.shape
    shapes = [(places, rows, columns // 3), (rows, columns // 3), (rows, columns // 3)]
    whole = lambda shape: pl.BlockSpec(shape, lambda i: (0,) * len(shape))
    return pl.pallas_call(
        plane_kernel,
        grid=(1,),
        in_specs=[whole(arrived.shape)],
        out_specs=[whole(shape) for shape in shapes],
        out_shape=[jax.ShapeDtypeStruct(shape, BF16) for shape in shapes],
        compiler_params=pltpu.CompilerParams(vmem_limit_bytes=32 * 1024 * 1024),
        name="plane_parts",
    )(arrived)


def pair_kernel(token_pair, token_far, own, other, gate, up):
    quarter, units = token_pair.shape[0] // 2, gate.shape[1]

    def product(columns):
        total = None
        for core, grads in enumerate((own, other)):
            for x_hi, tokens in enumerate((token_pair, token_far)):
                right = grads[:, x_hi, :, columns].reshape(quarter, units)
                term = dot_tn(tokens[core * quarter : (core + 1) * quarter], right)
                total = term if total is None else total + term
        return total

    gate[...] = product(slice(0, units))
    up[...] = product(slice(units, 2 * units))


def pair_grads(token_pair, token_far, own, other):
    width, units = token_pair.shape[1], own.shape[3] // 2
    step = width // 2
    tokens = pl.BlockSpec((token_pair.shape[0], step), lambda i: (0, i))
    grads = pl.BlockSpec(own.shape, lambda i: (0, 0, 0, 0))
    return pl.pallas_call(
        pair_kernel,
        grid=(2,),
        in_specs=[tokens, tokens, grads, grads],
        out_specs=[pl.BlockSpec((step, units), lambda i: (i, 0))] * 2,
        out_shape=[jax.ShapeDtypeStruct((width, units), F32)] * 2,
        compiler_params=pltpu.CompilerParams(vmem_limit_bytes=32 * 1024 * 1024),
        cost_estimate=pl.CostEstimate(
            flops=8 * token_pair.shape[0] * width * units,
            bytes_accessed=4 * token_pair.shape[0] * (width + 2 * units) + 8 * width * units,
            transcendentals=0,
        ),
        name="pair_grads",
    )(token_pair, token_far, own, other)


def on_device(
    tokens, cotangent, gate_codes, gate_scales, up_codes, up_scales, down_codes, down_scales
):
    seq_place = lax.axis_index(SEQ)
    tp_place = lax.axis_index(TP)
    core = lax.axis_index("core")
    rows, width = tokens.shape
    units = gate_codes.shape[1]
    half = rows // 2
    quarter = 16 * half

    place = jnp.stack([seq_place, tp_place]).astype(jnp.int32)
    w_near = dequantize(
        place, (gate_codes, up_codes, down_codes), (gate_scales, up_scales, down_scales.T)
    )
    w_near, tokens, cotangent = lax.optimization_barrier((w_near, tokens, cotangent))
    w_far = other_xh(w_near)
    w_near_other = other_core(w_near)

    halves = jnp.stack([tokens.reshape(2, half, width), cotangent.reshape(2, half, width)], axis=1)
    kept, got = pick(halves, core), other_core(pick(halves, 1 - core))
    mine = jnp.concatenate([kept[0], got[0], kept[1], got[1]], axis=1)
    body = 4 * width - LANES
    tail = lax.all_to_all(jnp.broadcast_to(mine[None, :, body:], (16, half, LANES)), Z, 0, 0, tiled=False)
    tail = tail.reshape(quarter, LANES)
    frames = lax.all_gather(mine[:, :body], Z, axis=0, tiled=True)
    w_far, frames, tail = lax.optimization_barrier((w_far, frames, tail))
    w_far_other = other_core(w_far)

    parts = forward_parts(frames, tail, w_near, w_far, w_near_other, w_far_other)
    parts, frames, tail = lax.optimization_barrier((parts, frames, tail))
    arrived = lax.all_to_all(parts.reshape(8, rows, 6 * units), PLANE, 0, 0, tiled=False)

    swap = other_core(jnp.concatenate([frames[:, width : 2 * width], frames[:, 3 * width :], tail], axis=1))
    token_pair = jnp.concatenate([frames[:, :width], swap[:, :width]])
    cot_pair = jnp.concatenate([frames[:, 2 * width : 3 * width], swap[:, width:]])
    hidden, kept, sent = plane_parts(arrived)
    hidden_own = lax.all_to_all(hidden, PLANE, 0, 0, tiled=False)

    got, hidden_own, token_far = lax.optimization_barrier((other_xh(sent), hidden_own, other_xh(token_pair)))
    grads_own = spread(jnp.stack([kept, got]), 8).reshape(8, 2, rows, 2 * units)

    hidden_own = hidden_own.reshape(quarter, 2 * units)
    hidden_other = other_core(hidden_own)
    w_down_pair = jnp.concatenate([w_near[2], w_far[2]])
    mixed = jnp.stack(
        [dot(hidden_own, w_down_pair).astype(BF16), dot(hidden_other, w_down_pair).astype(BF16)]
    )
    mixed = mixed.reshape(2, 16, half, width).transpose(1, 0, 2, 3).reshape(16, rows, width)
    mixed = halved(mixed, lax.axis_index("zn"), [(i, i ^ 1) for i in range(16)])
    units_pair = jnp.concatenate([hidden_own[:, :units], hidden_other[:, :units]])
    units_far = other_xh(jnp.concatenate([hidden_own[:, units:], hidden_other[:, units:]]))
    grads_own, mixed, cot_pair, units_far = lax.optimization_barrier((grads_own, mixed, cot_pair, units_far))
    cot_far = other_xh(cot_pair)
    grads_other = other_core(grads_own)
    mixed = summed(mixed, ("zh", "zm")).reshape(2, half, width)
    mixed = jnp.where(core == 0, mixed, mixed[::-1]).astype(BF16).reshape(rows, width)

    mixed, cot_far = lax.optimization_barrier((mixed, cot_far))

    grad_gate, grad_up = pair_grads(token_pair, token_far, grads_own, grads_other)
    grad_down = dot_tn(units_pair, cot_pair) + dot_tn(units_far, cot_far)
    return (mixed, grad_gate, grad_up, grad_down)


def solution(mesh):
    named = Mesh(mesh.devices.reshape(SIZES), SEQ + TP)
    return jax.shard_map(
        on_device,
        mesh=named,
        in_specs=(
            P(TP, SEQ),
            P(TP, SEQ),
            P(SEQ, TP),
            P(),
            P(SEQ, TP),
            P(),
            P(TP, SEQ),
            P(),
        ),
        out_specs=(P(TP, SEQ), P(SEQ, TP), P(SEQ, TP), P(TP, SEQ)),
        check_vma=False,
    )
```

time: 203 us -> 194 us (0.956)
  blocking collectives: 69.7 us -> 36.2 us
  starting transfers between devices: 50.9 us -> 73.7 us
  waiting for transfers between devices: 33.7 us -> 48 us
  Pallas kernels: 2.21 us -> 12.6 us
  matrix products: 14.4 us -> 6.2 us
  local copies, waits for them, and re-layouts: 17.3 us -> 9.77 us
  other arithmetic: 11 us -> 5.01 us
    all_gather x2 -> x1, blocking collectives: 69.7 us -> 36.2 us  [on_device(): frames = lax.all_gather(mine[:, :body], Z, axis=0, tiled=True)]
    all_to_all x1 -> x3, starting transfers between devices: 5.44 us -> 24.6 us  [the longest x1 15.2 us: on_device(): lax.all_to_all(jnp.broadcast_to(mine[None, :, body:], (16, half, LANES)),...]
    ppermute x10 -> x11, waiting for transfers between devices: 3.41 us -> 14 us  [shift(): return lax.ppermute(x, axes, [(i, (i + by) % size) for i in range(size)])]
    pallas_call x2 -> x4, Pallas kernels: 2.21 us -> 12.6 us  [the longest x1 3.95 us: forward_parts(): pl.pallas_call(forward_kernel, grid=(count,), in_specs=[whole(frames), wh...]
    all_to_all x2 -> x1, waiting for transfers between devices: 24.8 us -> 15.3 us  [summed(): return lax.all_to_all(x, axes, 0, 0, tiled=False).astype(F32).sum(0)]
    dot_general x9 -> x2, matrix products: 12.5 us -> 3.09 us  [dot_tn(): lax.dot_general(a, b, (((0,), (0,)), ((), ())), preferred_element_type=F32)]
    ppermute x0 -> x1, waiting for transfers between devices: none -> 7.77 us  [halved(): lax.ppermute(away, Z, pairs).astype(F32)]
    all_to_all x1 -> x3, waiting for transfers between devices: 3.81 us -> 11 us  [the longest x1 11 us: on_device(): lax.all_to_all(parts.reshape(8, rows, 6 * units), PLANE, 0, 0, tiled=False)]
  transfers between devices with their start and end apart: 14 -> 17, of which waited for: 4 -> 8; matrix products, arithmetic and copies ran while one was open for 11% -> 10% of each run, Pallas kernels for 0% -> 1%
where the time goes in v2:
time: 194 us; the launch traced here: 192 us
  starting transfers between devices  73.7 us (38%)
  waiting for transfers between devices  48 us (25%)
  blocking collectives  36.2 us (19%)
  Pallas kernels  12.6 us (6%)
  local copies, waits for them, and re-layouts  9.77 us (5%)
  matrix products  6.2 us (3%)
  other arithmetic  5.01 us (3%)
    all_gather x1, blocking collectives, on_device(): frames = lax.all_gather(mine[:, :body], Z, axis=0, tiled=True)  36.2 us
    ppermute x11, starting transfers between devices, shift(): return lax.ppermute(x, axes, [(i, (i + by) % size) for i in range(size)])  32.8 us
    all_to_all x1, waiting for transfers between devices, summed(): return lax.all_to_all(x, axes, 0, 0, tiled=False).astype(F32).sum(0)  15.3 us
    all_to_all x1, starting transfers between devices, on_device(): lax.all_to_all(jnp.broadcast_to(mine[None, :, body:], (16, half, LANES)),...  15.2 us
    ppermute x11, waiting for transfers between devices, shift(): return lax.ppermute(x, axes, [(i, (i + by) % size) for i in range(size)])  14 us
    all_to_all x1, waiting for transfers between devices, on_device(): lax.all_to_all(parts.reshape(8, rows, 6 * units), PLANE, 0, 0, tiled=False)  11 us
    all_to_all x1, starting transfers between devices, summed(): return lax.all_to_all(x, axes, 0, 0, tiled=False).astype(F32).sum(0)  9.22 us
    ppermute x1, waiting for transfers between devices, halved(): lax.ppermute(away, Z, pairs).astype(F32)  7.77 us
  transfers between devices with their start and end apart: 17, of which 8 were waited for; matrix products, arithmetic and copies ran while one was open for 10% of the time, Pallas kernels for 1%

profile of v2, /device:TPU:24, one launch (start us, length us, event | category | flops | bytes accessed | tf_op | source)
XLA Modules:
  0.0 192.4 jit_solution(6436610998457681522)
XLA Ops:
  0.6 0.6 pad_add_fusion.place
  1.2 3.8 %dequantize.1.near = bf16[3,512,512]{2,1,0:T(8,128)(2,1)} custom-call(s32[2]{0:T(128)} %pad_add_fusion.place, f32[64,128]{1,0:T(8,128)} %gate_scales.1, f32[64,128]{1,0:T(8,128)} %up_scales.1, f32[64,128]{1,0:T(8,128)} %bitcast.58, bf16[512,512]{1,0:T(8,128)(2,1)} %gate.1, bf16[512,512]{1,0:T(8,128)(2,1)} %up.1, bf16[512,512]{1,0:T(8,128)(2,1)} %down.1), custom_call_target="tpu_custom_call" | custom-call | tf_op jit(solution)/shard_map/dequantize/pallas_call | solution.py:35
  5.1 5.1 %collective-permute-start = (bf16[3,512,512]{2,1,0:T(8,128)(2,1)}, bf16[3,512,512]{2,1,0:T(8,128)(2,1)}, u32[]{:S(2)}, u32[]{:S(2)}) collective-permute-start(bf16[3,512,512]{2,1,0:T(8,128)(2,1)} %dequantize.1.near), channel_id=1, source_target_pairs={{0,16},{16,0},{1,17},{17,1},{2,18},{18,2},{3,19},{19,3},{4,20},{20... | collective-permute-start | bytes 4718600 | tf_op jit(solution)/shard_map/ppermute | solution.py:50
  10.1 1.9 collective-permute-start.2
  12.1 0.0 copy-done.9
  12.1 2.4 %collective-permute-start.1 = (bf16[2,16,512]{2,1,0:T(8,128)(2,1)S(1)}, bf16[2,16,512]{2,1,0:T(8,128)(2,1)S(1)}, u32[]{:S(2)}, u32[]{:S(2)}) collective-permute-start(bf16[2,16,512]{2,1,0:T(8,128)(2,1)S(1)} %get-tuple-element.60), channel_id=1, source_target_pairs={{0,32},{32,0},{1,33},{33,1},{2,34},{34,2},{3,35},{35,3},{4,36},{36... | collective-permute-start | bytes 98312 | tf_op jit(solution)/shard_map/ppermute | solution.py:50
  14.5 0.9 collective-permute-done.1
  15.5 0.6 broadcast_in_dim.4
  16.1 15.2 %all-to-all-start = ((bf16[16,16,128]{2,1,0:T(8,128)(2,1)}), bf16[16,16,128]{2,1,0:T(8,128)(2,1)S(1)}, u32[]{:S(2)}, u32[]{:S(2)}) async-start(bf16[16,16,128]{2,1,0:T(8,128)(2,1)} %broadcast_in_dim.4), calls=%async_computation | async-start | bytes 131072 | tf_op jit(solution)/shard_map/all_to_all | solution.py:219
  31.4 36.2 %all_gather.3.frames = bf16[256,1920]{1,0:T(8,128)(2,1)S(1)} all-gather(bf16[16,1920]{1,0:T(8,128)(2,1)S(1)} %pad_maximum_fusion.9), channel_id=1, replica_groups=mesh['xl'=2,'y'=4,'core'=2,'xh'=2,'zh'=4,'zm'=2,'zn'=2] {'zh','zm','zn'}, dimensions={0}, use_global_device_ids=true | all-gather | bytes 1044480 | tf_op jit(solution)/shard_map/all_gather | solution.py:221
  67.5 0.0 all-to-all-done
  67.5 0.0 collective-permute-done.far
  67.6 1.9 collective-permute-start.3
  69.5 0.0 collective-permute-done.2.near_other
  69.5 3.6 %collective-permute-done.3.far_other = bf16[3,512,512]{2,1,0:T(8,128)(2,1)S(1)} collective-permute-done((bf16[3,512,512]{2,1,0:T(8,128)(2,1)}, bf16[3,512,512]{2,1,0:T(8,128)(2,1)S(1)}, u32[]{:S(2)}, u32[]{:S(2)}) %collective-permute-start.3) | collective-permute-done | bytes 1572896 | tf_op jit(solution)/shard_map/ppermute | solution.py:50
  73.1 4.0 %forward_parts.1 = bf16[256,3072]{1,0:T(8,128)(2,1)S(1)} custom-call(bf16[256,1920]{1,0:T(8,128)(2,1)S(1)} %all_gather.3.frames, bf16[256,128]{1,0:T(8,128)(2,1)S(1)} %bitcast.46, bf16[3,512,512]{2,1,0:T(8,128)(2,1)S(1)} %copy-done, bf16[3,512,512]{2,1,0:T(8,128)(2,1)} %collective-permute-done.far, bf16[3,512,512]{2,1,0:T(8,128)(2,1)} %collective-permute-done.2.near_other, ...), custom_call_target="tpu_custom_call" | custom-call | flops 1610612736 | bytes 7864320 | tf_op jit(solution)/shard_map/forward_parts/pallas_call | solution.py:114
  77.0 1.1 copy-done.1
  78.2 4.9 %all-to-all-start.1 = ((bf16[8,32,3072]{2,1,0:T(8,128)(2,1)}), bf16[8,32,3072]{2,1,0:T(8,128)(2,1)}, u32[]{:S(2)}, u32[]{:S(2)}) async-start(bf16[8,32,3072]{2,1,0:T(8,128)(2,1)} %bitcast.45), calls=%async_computation.1 | async-start | bytes 3145728 | tf_op jit(solution)/shard_map/all_to_all | solution.py:227
  83.0 0.8 fusion.11
  83.8 0.1 pad_maximum_fusion.3
  83.9 1.9 collective-permute-start.5
  85.8 1.9 collective-permute-done.5
  87.7 0.7 fusion.14
  88.5 4.2 %collective-permute-start.6 = (bf16[512,512]{1,0:T(8,128)(2,1)S(1)}, bf16[512,512]{1,0:T(8,128)(2,1)S(1)}, u32[]{:S(2)}, u32[]{:S(2)}) collective-permute-start(bf16[512,512]{1,0:T(8,128)(2,1)S(1)} %pad_maximum_fusion.4.token_pair), channel_id=1, source_target_pairs={{0,16},{16,0},{1,17},{17,1},{2,18},{18,2},{3,19},{19,3},{4,20},{20... | collective-permute-start | bytes 1572872 | tf_op jit(solution)/shard_map/ppermute | solution.py:50
  92.6 11.0 %all-to-all-done.1.arrived = bf16[8,32,3072]{2,1,0:T(8,128)(2,1)} async-done(((bf16[8,32,3072]{2,1,0:T(8,128)(2,1)}), bf16[8,32,3072]{2,1,0:T(8,128)(2,1)}, u32[]{:S(2)}, u32[]{:S(2)}) %all-to-all-start.1) | async-done | bytes 1572896 | tf_op jit(solution)/shard_map/all_to_all | solution.py:227
  103.6 2.4 %plane_parts.1 = (bf16[8,32,1024]{2,1,0:T(8,128)(2,1)}, bf16[32,1024]{1,0:T(8,128)(2,1)S(1)}, bf16[32,1024]{1,0:T(8,128)(2,1)S(1)}) custom-call(bf16[8,32,3072]{2,1,0:T(8,128)(2,1)} %all-to-all-done.1.arrived), custom_call_target="tpu_custom_call" | custom-call | tf_op jit(solution)/shard_map/plane_parts/pallas_call | solution.py:148
  106.0 4.5 %all-to-all-start.2 = ((bf16[8,32,1024]{2,1,0:T(8,128)(2,1)}), bf16[8,32,1024]{2,1,0:T(8,128)(2,1)S(1)}, u32[]{:S(2)}, u32[]{:S(2)}) async-start(bf16[8,32,1024]{2,1,0:T(8,128)(2,1)} %get-tuple-element.36), calls=%async_computation.2 | async-start | bytes 1048576 | tf_op jit(solution)/shard_map/all_to_all | solution.py:233
  110.5 0.8 slice_bitcast_fusion.1
  111.3 4.1 %collective-permute-start.4 = (bf16[32,1024]{1,0:T(8,128)(2,1)S(1)}, bf16[32,1024]{1,0:T(8,128)(2,1)S(1)}, u32[]{:S(2)}, u32[]{:S(2)}) collective-permute-start(bf16[32,1024]{1,0:T(8,128)(2,1)S(1)} %get-tuple-element.35), channel_id=1, source_target_pairs={{0,16},{16,0},{1,17},{17,1},{2,18},{18,2},{3,19},{19,3},{4,20},{20... | collective-permute-start | bytes 196616 | tf_op jit(solution)/shard_map/ppermute | solution.py:50
  115.5 1.9 slice_bitcast_fusion
  117.4 0.0 collective-permute-done.6.token_far
  117.4 4.1 %collective-permute-done.4 = bf16[32,1024]{1,0:T(8,128)(2,1)S(1)} collective-permute-done((bf16[32,1024]{1,0:T(8,128)(2,1)S(1)}, bf16[32,1024]{1,0:T(8,128)(2,1)S(1)}, u32[]{:S(2)}, u32[]{:S(2)}) %collective-permute-start.4) | collective-permute-done | bytes 65568 | tf_op jit(solution)/shard_map/ppermute | solution.py:50
  121.5 0.0 all-to-all-done.2
  121.5 1.9 collective-permute-start.7
  123.4 1.1 broadcast_in_dim.5
  124.5 4.8 %all-to-all-start.3 = ((bf16[8,2,32,1024]{3,2,1,0:T(8,128)(2,1)}), bf16[8,2,32,1024]{3,2,1,0:T(8,128)(2,1)S(1)}, u32[]{:S(2)}, u32[]{:S(2)}) async-start(bf16[8,2,32,1024]{3,2,1,0:T(8,128)(2,1)} %broadcast_in_dim.5), calls=%async_computation.3 | async-start | bytes 2097152 | tf_op jit(solution)/shard_map/all_to_all | solution.py:89
  129.4 1.6 convolution_convert_fusion.1
  131.0 0.0 copy-start.7
  131.0 0.0 copy-start.8
  131.0 0.0 collective-permute-done.7
  131.0 1.9 fusion.13
  132.9 0.8 pad_maximum_fusion.7
  133.7 4.5 %collective-permute-start.9 = (bf16[512,512]{1,0:T(8,128)(2,1)}, bf16[512,512]{1,0:T(8,128)(2,1)}, u32[]{:S(2)}, u32[]{:S(2)}) collective-permute-start(bf16[512,512]{1,0:T(8,128)(2,1)} %pad_maximum_fusion.7), channel_id=1, source_target_pairs={{0,16},{16,0},{1,17},{17,1},{2,18},{18,2},{3,19},{19,3},{4,20},{20... | collective-permute-start | bytes 1572872 | tf_op jit(solution)/shard_map/ppermute | solution.py:50
  138.3 1.5 convolution_convert_fusion
  139.7 0.1 pad_maximum_fusion.5
  139.8 0.7 dynamic-slice_bitcast_fusion
  140.5 2.2 %collective-permute-start.8 = (bf16[8,32,512]{2,1,0:T(8,128)(2,1)}, bf16[8,32,512]{2,1,0:T(8,128)(2,1)}, u32[]{:S(2)}, u32[]{:S(2)}) collective-permute-start(bf16[8,32,512]{2,1,0:T(8,128)(2,1)} %dynamic-slice_bitcast_fusion), channel_id=1, source_target_pairs={{0,1},{1,0},{2,3},{3,2},{4,5},{5,4},{6,7},{7,6},{8,9},{9,8},{10,11... | collective-permute-start | bytes 786440 | tf_op jit(solution)/shard_map/ppermute | solution.py:84
  142.8 7.8 %collective-permute-done.8 = bf16[8,32,512]{2,1,0:T(8,128)(2,1)} collective-permute-done((bf16[8,32,512]{2,1,0:T(8,128)(2,1)}, bf16[8,32,512]{2,1,0:T(8,128)(2,1)}, u32[]{:S(2)}, u32[]{:S(2)}) %collective-permute-start.8) | collective-permute-done | bytes 262176 | tf_op jit(solution)/shard_map/ppermute | solution.py:84
  150.6 1.7 fusion.3
  152.3 0.0 all-to-all-done.3.own
  152.3 3.5 %collective-permute-done.9 = bf16[512,512]{1,0:T(8,128)(2,1)} collective-permute-done((bf16[512,512]{1,0:T(8,128)(2,1)}, bf16[512,512]{1,0:T(8,128)(2,1)}, u32[]{:S(2)}, u32[]{:S(2)}) %collective-permute-start.9) | collective-permute-done | bytes 524320 | tf_op jit(solution)/shard_map/ppermute | solution.py:50
  155.8 9.2 %all-to-all-start.4 = ((bf16[8,32,512]{2,1,0:T(8,128)(2,1)}), bf16[8,32,512]{2,1,0:T(8,128)(2,1)}, u32[]{:S(2)}, u32[]{:S(2)}) async-start(bf16[8,32,512]{2,1,0:T(8,128)(2,1)} %fusion.3), calls=%async_computation.4 | async-start | bytes 524288 | tf_op jit(solution)/shard_map/all_to_all | solution.py:78
  165.0 2.9 %collective-permute-start.10 = (bf16[512,512]{1,0:T(8,128)(2,1)S(1)}, bf16[512,512]{1,0:T(8,128)(2,1)}, u32[]{:S(2)}, u32[]{:S(2)}) collective-permute-start(bf16[512,512]{1,0:T(8,128)(2,1)S(1)} %pad_maximum_fusion.6), channel_id=1, source_target_pairs={{0,16},{16,0},{1,17},{17,1},{2,18},{18,2},{3,19},{19,3},{4,20},{20... | collective-permute-start | bytes 1572872 | tf_op jit(solution)/shard_map/ppermute | solution.py:50
  168.0 1.9 collective-permute-start.11
  169.9 15.3 %all-to-all-done.4 = bf16[8,32,512]{2,1,0:T(8,128)(2,1)} async-done(((bf16[8,32,512]{2,1,0:T(8,128)(2,1)}), bf16[8,32,512]{2,1,0:T(8,128)(2,1)}, u32[]{:S(2)}, u32[]{:S(2)}) %all-to-all-start.4) | async-done | bytes 262176 | tf_op jit(solution)/shard_map/all_to_all | solution.py:78
  185.2 1.0 convert_reduce_fusion
  186.2 0.6 fusion.4
  186.8 0.0 collective-permute-done.10
  186.8 1.7 fusion.15
  188.5 0.0 copy-done.4
  188.5 0.0 copy-start.3
  188.5 1.4 convolution_add_fusion
  190.0 0.0 collective-permute-done.11.other
  190.0 2.4 %pair_grads.1 = (f32[512,512]{1,0:T(8,128)}, f32[512,512]{1,0:T(8,128)}) custom-call(bf16[512,512]{1,0:T(8,128)(2,1)S(1)} %pad_maximum_fusion.4.token_pair, bf16[512,512]{1,0:T(8,128)(2,1)S(1)} %copy-done.3, bf16[8,2,32,1024]{3,2,1,0:T(8,128)(2,1)S(1)} %all-to-all-done.3.own, bf16[8,2,32,1024]{3,2,1,0:T(8,128)(2,1)S(1)} %collective-permute-done.11.other), custom_call_target="tpu_custom_call" | custom-call | flops 1073741824 | bytes 5242880 | tf_op jit(solution)/shard_map/pair_grads/pallas_call | solution.py:180
  (26 shorter events, 0.2 us)
Async XLA Ops:
  1.2 10.8 %copy-start.9 = (bf16[32,512]{1,0:T(8,128)(2,1)S(1)}, bf16[32,512]{1,0:T(8,128)(2,1)}, u32[]{:S(2)}) copy-start(bf16[32,512]{1,0:T(8,128)(2,1)} %param.8) | copy-start | bytes 98308
  1.2 10.8 %copy-start.10 = (bf16[32,512]{1,0:T(8,128)(2,1)S(1)}, bf16[32,512]{1,0:T(8,128)(2,1)}, u32[]{:S(2)}) copy-start(bf16[32,512]{1,0:T(8,128)(2,1)} %param.9) | copy-start | bytes 98308
  5.1 68.0 %copy-start = (bf16[3,512,512]{2,1,0:T(8,128)(2,1)S(1)}, bf16[3,512,512]{2,1,0:T(8,128)(2,1)}, u32[]{:S(2)}) copy-start(bf16[3,512,512]{2,1,0:T(8,128)(2,1)} %dequantize.1.near) | copy-start | bytes 4718596
  5.1 62.5 %collective-permute-start = (bf16[3,512,512]{2,1,0:T(8,128)(2,1)}, bf16[3,512,512]{2,1,0:T(8,128)(2,1)}, u32[]{:S(2)}, u32[]{:S(2)}) collective-permute-start(bf16[3,512,512]{2,1,0:T(8,128)(2,1)} %dequantize.1.near), channel_id=1, source_target_pairs={{0,16},{16,0},{1,17},{17,1},{2,18},{18,2},{3,19},{19,3},{4,20},{20... | collective-permute-start | bytes 4718600 | tf_op jit(solution)/shard_map/ppermute | solution.py:50
  10.1 59.3 %collective-permute-start.2 = (bf16[3,512,512]{2,1,0:T(8,128)(2,1)}, bf16[3,512,512]{2,1,0:T(8,128)(2,1)}, u32[]{:S(2)}, u32[]{:S(2)}) collective-permute-start(bf16[3,512,512]{2,1,0:T(8,128)(2,1)} %dequantize.1.near), channel_id=1, source_target_pairs={{0,32},{32,0},{1,33},{33,1},{2,34},{34,2},{3,35},{35,3},{4,36},{36... | collective-permute-start | bytes 4718600 | tf_op jit(solution)/shard_map/ppermute | solution.py:50
  12.1 3.4 %collective-permute-start.1 = (bf16[2,16,512]{2,1,0:T(8,128)(2,1)S(1)}, bf16[2,16,512]{2,1,0:T(8,128)(2,1)S(1)}, u32[]{:S(2)}, u32[]{:S(2)}) collective-permute-start(bf16[2,16,512]{2,1,0:T(8,128)(2,1)S(1)} %get-tuple-element.60), channel_id=1, source_target_pairs={{0,32},{32,0},{1,33},{33,1},{2,34},{34,2},{3,35},{35,3},{4,36},{36... | collective-permute-start | bytes 98312 | tf_op jit(solution)/shard_map/ppermute | solution.py:50
  16.1 51.4 %all-to-all-start = ((bf16[16,16,128]{2,1,0:T(8,128)(2,1)}), bf16[16,16,128]{2,1,0:T(8,128)(2,1)S(1)}, u32[]{:S(2)}, u32[]{:S(2)}) async-start(bf16[16,16,128]{2,1,0:T(8,128)(2,1)} %broadcast_in_dim.4), calls=%async_computation | async-start | bytes 131072 | tf_op jit(solution)/shard_map/all_to_all | solution.py:219
  67.6 5.5 %collective-permute-start.3 = (bf16[3,512,512]{2,1,0:T(8,128)(2,1)}, bf16[3,512,512]{2,1,0:T(8,128)(2,1)S(1)}, u32[]{:S(2)}, u32[]{:S(2)}) collective-permute-start(bf16[3,512,512]{2,1,0:T(8,128)(2,1)} %collective-permute-done.far), channel_id=1, source_target_pairs={{0,32},{32,0},{1,33},{33,1},{2,34},{34,2},{3,35},{35,3},{4,36},{36... | collective-permute-start | bytes 4718600 | tf_op jit(solution)/shard_map/ppermute | solution.py:50
  77.0 1.1 copy-start.1
  78.2 25.4 %all-to-all-start.1 = ((bf16[8,32,3072]{2,1,0:T(8,128)(2,1)}), bf16[8,32,3072]{2,1,0:T(8,128)(2,1)}, u32[]{:S(2)}, u32[]{:S(2)}) async-start(bf16[8,32,3072]{2,1,0:T(8,128)(2,1)} %bitcast.45), calls=%async_computation.1 | async-start | bytes 3145728 | tf_op jit(solution)/shard_map/all_to_all | solution.py:227
  83.9 3.8 %collective-permute-start.5 = (bf16[256,1024]{1,0:T(8,128)(2,1)S(1)}, bf16[256,1024]{1,0:T(8,128)(2,1)S(1)}, u32[]{:S(2)}, u32[]{:S(2)}) collective-permute-start(bf16[256,1024]{1,0:T(8,128)(2,1)S(1)} %pad_maximum_fusion.3), channel_id=1, source_target_pairs={{0,32},{32,0},{1,33},{33,1},{2,34},{34,2},{3,35},{35,3},{4,36},{36... | collective-permute-start | bytes 1572872 | tf_op jit(solution)/shard_map/ppermute | solution.py:50
  88.5 28.9 %collective-permute-start.6 = (bf16[512,512]{1,0:T(8,128)(2,1)S(1)}, bf16[512,512]{1,0:T(8,128)(2,1)S(1)}, u32[]{:S(2)}, u32[]{:S(2)}) collective-permute-start(bf16[512,512]{1,0:T(8,128)(2,1)S(1)} %pad_maximum_fusion.4.token_pair), channel_id=1, source_target_pairs={{0,16},{16,0},{1,17},{17,1},{2,18},{18,2},{3,19},{19,3},{4,20},{20... | collective-permute-start | bytes 1572872 | tf_op jit(solution)/shard_map/ppermute | solution.py:50
  106.0 15.5 %all-to-all-start.2 = ((bf16[8,32,1024]{2,1,0:T(8,128)(2,1)}), bf16[8,32,1024]{2,1,0:T(8,128)(2,1)S(1)}, u32[]{:S(2)}, u32[]{:S(2)}) async-start(bf16[8,32,1024]{2,1,0:T(8,128)(2,1)} %get-tuple-element.36), calls=%async_computation.2 | async-start | bytes 1048576 | tf_op jit(solution)/shard_map/all_to_all | solution.py:233
  111.3 10.1 %collective-permute-start.4 = (bf16[32,1024]{1,0:T(8,128)(2,1)S(1)}, bf16[32,1024]{1,0:T(8,128)(2,1)S(1)}, u32[]{:S(2)}, u32[]{:S(2)}) collective-permute-start(bf16[32,1024]{1,0:T(8,128)(2,1)S(1)} %get-tuple-element.35), channel_id=1, source_target_pairs={{0,16},{16,0},{1,17},{17,1},{2,18},{18,2},{3,19},{19,3},{4,20},{20... | collective-permute-start | bytes 196616 | tf_op jit(solution)/shard_map/ppermute | solution.py:50
  117.4 7.1 %copy-start.2 = (bf16[512,512]{1,0:T(8,128)(2,1)}, bf16[512,512]{1,0:T(8,128)(2,1)S(1)}, u32[]{:S(2)}) copy-start(bf16[512,512]{1,0:T(8,128)(2,1)S(1)} %collective-permute-done.6.token_far) | copy-start | bytes 1572868
  121.5 9.6 %collective-permute-start.7 = (bf16[256,1024]{1,0:T(8,128)(2,1)S(1)}, bf16[256,1024]{1,0:T(8,128)(2,1)}, u32[]{:S(2)}, u32[]{:S(2)}) collective-permute-start(bf16[256,1024]{1,0:T(8,128)(2,1)S(1)} %bitcast.49), channel_id=1, source_target_pairs={{0,32},{32,0},{1,33},{33,1},{2,34},{34,2},{3,35},{35,3},{4,36},{36... | collective-permute-start | bytes 1572872 | tf_op jit(solution)/shard_map/ppermute | solution.py:50
  124.5 27.8 %all-to-all-start.3 = ((bf16[8,2,32,1024]{3,2,1,0:T(8,128)(2,1)}), bf16[8,2,32,1024]{3,2,1,0:T(8,128)(2,1)S(1)}, u32[]{:S(2)}, u32[]{:S(2)}) async-start(bf16[8,2,32,1024]{3,2,1,0:T(8,128)(2,1)} %broadcast_in_dim.5), calls=%async_computation.3 | async-start | bytes 2097152 | tf_op jit(solution)/shard_map/all_to_all | solution.py:89
  131.0 7.2 %copy-start.7 = (bf16[512,512]{1,0:T(8,128)(2,1)S(1)}, bf16[512,512]{1,0:T(8,128)(2,1)}, u32[]{:S(2)}) copy-start(bf16[512,512]{1,0:T(8,128)(2,1)} %slice_bitcast_fusion.1) | copy-start | bytes 1572868
  131.0 7.2 %copy-start.8 = (bf16[512,512]{1,0:T(8,128)(2,1)S(1)}, bf16[512,512]{1,0:T(8,128)(2,1)}, u32[]{:S(2)}) copy-start(bf16[512,512]{1,0:T(8,128)(2,1)} %slice_bitcast_fusion) | copy-start | bytes 1572868
  133.7 9.1 %copy-start.5 = (bf16[256,512]{1,0:T(8,128)(2,1)S(1)}, bf16[256,512]{1,0:T(8,128)(2,1)}, u32[]{:S(2)}) copy-start(bf16[256,512]{1,0:T(8,128)(2,1)} %get-tuple-element.50) | copy-start | bytes 786436
  133.7 9.1 %copy-start.6 = (bf16[256,512]{1,0:T(8,128)(2,1)S(1)}, bf16[256,512]{1,0:T(8,128)(2,1)}, u32[]{:S(2)}) copy-start(bf16[256,512]{1,0:T(8,128)(2,1)} %get-tuple-element.57) | copy-start | bytes 786436
  133.7 22.1 %collective-permute-start.9 = (bf16[512,512]{1,0:T(8,128)(2,1)}, bf16[512,512]{1,0:T(8,128)(2,1)}, u32[]{:S(2)}, u32[]{:S(2)}) collective-permute-start(bf16[512,512]{1,0:T(8,128)(2,1)} %pad_maximum_fusion.7), channel_id=1, source_target_pairs={{0,16},{16,0},{1,17},{17,1},{2,18},{18,2},{3,19},{19,3},{4,20},{20... | collective-permute-start | bytes 1572872 | tf_op jit(solution)/shard_map/ppermute | solution.py:50
  140.5 10.1 %collective-permute-start.8 = (bf16[8,32,512]{2,1,0:T(8,128)(2,1)}, bf16[8,32,512]{2,1,0:T(8,128)(2,1)}, u32[]{:S(2)}, u32[]{:S(2)}) collective-permute-start(bf16[8,32,512]{2,1,0:T(8,128)(2,1)} %dynamic-slice_bitcast_fusion), channel_id=1, source_target_pairs={{0,1},{1,0},{2,3},{3,2},{4,5},{5,4},{6,7},{7,6},{8,9},{9,8},{10,11... | collective-permute-start | bytes 786440 | tf_op jit(solution)/shard_map/ppermute | solution.py:84
  155.8 29.4 %all-to-all-start.4 = ((bf16[8,32,512]{2,1,0:T(8,128)(2,1)}), bf16[8,32,512]{2,1,0:T(8,128)(2,1)}, u32[]{:S(2)}, u32[]{:S(2)}) async-start(bf16[8,32,512]{2,1,0:T(8,128)(2,1)} %fusion.3), calls=%async_computation.4 | async-start | bytes 524288 | tf_op jit(solution)/shard_map/all_to_all | solution.py:78
  165.0 21.8 %collective-permute-start.10 = (bf16[512,512]{1,0:T(8,128)(2,1)S(1)}, bf16[512,512]{1,0:T(8,128)(2,1)}, u32[]{:S(2)}, u32[]{:S(2)}) collective-permute-start(bf16[512,512]{1,0:T(8,128)(2,1)S(1)} %pad_maximum_fusion.6), channel_id=1, source_target_pairs={{0,16},{16,0},{1,17},{17,1},{2,18},{18,2},{3,19},{19,3},{4,20},{20... | collective-permute-start | bytes 1572872 | tf_op jit(solution)/shard_map/ppermute | solution.py:50
  168.0 22.0 %collective-permute-start.11 = (bf16[8,2,32,1024]{3,2,1,0:T(8,128)(2,1)S(1)}, bf16[8,2,32,1024]{3,2,1,0:T(8,128)(2,1)S(1)}, u32[]{:S(2)}, u32[]{:S(2)}) collective-permute-start(bf16[8,2,32,1024]{3,2,1,0:T(8,128)(2,1)S(1)} %all-to-all-done.3.own), channel_id=1, source_target_pairs={{0,32},{32,0},{1,33},{33,1},{2,34},{34,2},{3,35},{35,3},{4,36},{36... | collective-permute-start | bytes 3145736 | tf_op jit(solution)/shard_map/ppermute | solution.py:50
  185.2 3.3 %copy-start.4 = (bf16[256,512]{1,0:T(8,128)(2,1)S(1)}, bf16[256,512]{1,0:T(8,128)(2,1)}, u32[]{:S(2)}) copy-start(bf16[256,512]{1,0:T(8,128)(2,1)} %get-tuple-element.55) | copy-start | bytes 786436
  188.5 1.4 copy-start.3

commit v3 on v2

--- a/solution.py
+++ b/solution.py
@@ -72,10 +72,6 @@
 
 def dot_tn(a, b):
     return lax.dot_general(a, b, (((0,), (0,)), ((), ())), preferred_element_type=F32)
-
-
-def summed(x, axes):
-    return lax.all_to_all(x, axes, 0, 0, tiled=False).astype(F32).sum(0)
 
 
 def halved(x, place, pairs):
@@ -248,12 +244,14 @@
     grads_own, mixed, cot_pair, units_far = lax.optimization_barrier((grads_own, mixed, cot_pair, units_far))
     cot_far = other_xh(cot_pair)
     grads_other = other_core(grads_own)
-    mixed = summed(mixed, ("zh", "zm")).reshape(2, half, width)
+    landed = lax.all_to_all(mixed, ("zh", "zm"), 0, 0, tiled=False)
+    grad_gate, grad_up = pair_grads(token_pair, token_far, grads_own, grads_other)
+    landed, grad_gate, grad_up = lax.optimization_barrier((landed, grad_gate, grad_up))
+    mixed = landed.astype(F32).sum(0).reshape(2, half, width)
     mixed = jnp.where(core == 0, mixed, mixed[::-1]).astype(BF16).reshape(rows, width)
 
     mixed, cot_far = lax.optimization_barrier((mixed, cot_far))
 
-    grad_gate, grad_up = pair_grads(token_pair, token_far, grads_own, grads_other)
     grad_down = dot_tn(units_pair, cot_pair) + dot_tn(units_far, cot_far)
     return (mixed, grad_gate, grad_up, grad_down)
 

time: 194 us -> 195 us (level)
  transfers between devices with their start and end apart: 17 -> 17, of which waited for: 8 -> 8; matrix products, arithmetic and copies ran while one was open for 10% -> 9% of each run, Pallas kernels for 1% -> 2%
where the time goes in v3:
time: 195 us; the launch traced here: 193 us
  starting transfers between devices  73.7 us (38%)
  waiting for transfers between devices  47.7 us (24%)
  blocking collectives  36.2 us (19%)
  Pallas kernels  12.5 us (6%)
  local copies, waits for them, and re-layouts  9.8 us (5%)
  matrix products  6.19 us (3%)
  other arithmetic  5.79 us (3%)
    all_gather x1, blocking collectives, on_device(): frames = lax.all_gather(mine[:, :body], Z, axis=0, tiled=True)  36.2 us
    ppermute x11, starting transfers between devices, shift(): return lax.ppermute(x, axes, [(i, (i + by) % size) for i in range(size)])  32.8 us
    all_to_all x1, waiting for transfers between devices, on_device(): landed = lax.all_to_all(mixed, ('zh', 'zm'), 0, 0, tiled=False)  15.8 us
    all_to_all x1, starting transfers between devices, on_device(): lax.all_to_all(jnp.broadcast_to(mine[None, :, body:], (16, half, LANES)),...  15.2 us
    ppermute x11, waiting for transfers between devices, shift(): return lax.ppermute(x, axes, [(i, (i + by) % size) for i in range(size)])  13.9 us
    all_to_all x1, waiting for transfers between devices, on_device(): lax.all_to_all(parts.reshape(8, rows, 6 * units), PLANE, 0, 0, tiled=False)  10.9 us
    all_to_all x1, starting transfers between devices, on_device(): landed = lax.all_to_all(mixed, ('zh', 'zm'), 0, 0, tiled=False)  9.22 us
    ppermute x1, waiting for transfers between devices, halved(): lax.ppermute(away, Z, pairs).astype(F32)  6.99 us
  transfers between devices with their start and end apart: 17, of which 8 were waited for; matrix products, arithmetic and copies ran while one was open for 9% of the time, Pallas kernels for 2%

profile of v3, /device:TPU:24, one launch (start us, length us, event | category | flops | bytes accessed | tf_op | source)
XLA Modules:
  0.0 192.8 jit_solution(18258695802644566717)
XLA Ops:
  0.6 0.6 pad_add_fusion.place
  1.2 3.8 %dequantize.1.near = bf16[3,512,512]{2,1,0:T(8,128)(2,1)} custom-call(s32[2]{0:T(128)} %pad_add_fusion.place, f32[64,128]{1,0:T(8,128)} %gate_scales.1, f32[64,128]{1,0:T(8,128)} %up_scales.1, f32[64,128]{1,0:T(8,128)} %bitcast.58, bf16[512,512]{1,0:T(8,128)(2,1)} %gate.1, bf16[512,512]{1,0:T(8,128)(2,1)} %up.1, bf16[512,512]{1,0:T(8,128)(2,1)} %down.1), custom_call_target="tpu_custom_call" | custom-call | tf_op jit(solution)/shard_map/dequantize/pallas_call | solution.py:35
  5.1 5.1 %collective-permute-start = (bf16[3,512,512]{2,1,0:T(8,128)(2,1)}, bf16[3,512,512]{2,1,0:T(8,128)(2,1)}, u32[]{:S(2)}, u32[]{:S(2)}) collective-permute-start(bf16[3,512,512]{2,1,0:T(8,128)(2,1)} %dequantize.1.near), channel_id=1, source_target_pairs={{0,16},{16,0},{1,17},{17,1},{2,18},{18,2},{3,19},{19,3},{4,20},{20... | collective-permute-start | bytes 4718600 | tf_op jit(solution)/shard_map/ppermute | solution.py:50
  10.1 1.9 collective-permute-start.2
  12.1 2.4 %collective-permute-start.1 = (bf16[2,16,512]{2,1,0:T(8,128)(2,1)S(1)}, bf16[2,16,512]{2,1,0:T(8,128)(2,1)S(1)}, u32[]{:S(2)}, u32[]{:S(2)}) collective-permute-start(bf16[2,16,512]{2,1,0:T(8,128)(2,1)S(1)} %get-tuple-element.66), channel_id=1, source_target_pairs={{0,32},{32,0},{1,33},{33,1},{2,34},{34,2},{3,35},{35,3},{4,36},{36... | collective-permute-start | bytes 98312 | tf_op jit(solution)/shard_map/ppermute | solution.py:50
  14.5 0.9 collective-permute-done.1
  15.5 0.6 broadcast_in_dim.4
  16.1 15.2 %all-to-all-start = ((bf16[16,16,128]{2,1,0:T(8,128)(2,1)}), bf16[16,16,128]{2,1,0:T(8,128)(2,1)S(1)}, u32[]{:S(2)}, u32[]{:S(2)}) async-start(bf16[16,16,128]{2,1,0:T(8,128)(2,1)} %broadcast_in_dim.4), calls=%async_computation | async-start | bytes 131072 | tf_op jit(solution)/shard_map/all_to_all | solution.py:215
  31.4 36.2 %all_gather.3.frames = bf16[256,1920]{1,0:T(8,128)(2,1)S(1)} all-gather(bf16[16,1920]{1,0:T(8,128)(2,1)S(1)} %pad_maximum_fusion.9), channel_id=1, replica_groups=mesh['xl'=2,'y'=4,'core'=2,'xh'=2,'zh'=4,'zm'=2,'zn'=2] {'zh','zm','zn'}, dimensions={0}, use_global_device_ids=true | all-gather | bytes 1044480 | tf_op jit(solution)/shard_map/all_gather | solution.py:217
  67.5 0.0 all-to-all-done
  67.5 0.0 collective-permute-done.far
  67.5 1.9 collective-permute-start.3
  69.5 0.0 collective-permute-done.2.near_other
  69.5 3.6 %collective-permute-done.3.far_other = bf16[3,512,512]{2,1,0:T(8,128)(2,1)S(1)} collective-permute-done((bf16[3,512,512]{2,1,0:T(8,128)(2,1)}, bf16[3,512,512]{2,1,0:T(8,128)(2,1)S(1)}, u32[]{:S(2)}, u32[]{:S(2)}) %collective-permute-start.3) | collective-permute-done | bytes 1572896 | tf_op jit(solution)/shard_map/ppermute | solution.py:50
  73.1 0.0 copy-done
  73.1 4.0 %forward_parts.1 = bf16[256,3072]{1,0:T(8,128)(2,1)S(1)} custom-call(bf16[256,1920]{1,0:T(8,128)(2,1)S(1)} %all_gather.3.frames, bf16[256,128]{1,0:T(8,128)(2,1)S(1)} %bitcast.46, bf16[3,512,512]{2,1,0:T(8,128)(2,1)S(1)} %copy-done, bf16[3,512,512]{2,1,0:T(8,128)(2,1)} %collective-permute-done.far, bf16[3,512,512]{2,1,0:T(8,128)(2,1)} %collective-permute-done.2.near_other, ...), custom_call_target="tpu_custom_call" | custom-call | flops 1610612736 | bytes 7864320 | tf_op jit(solution)/shard_map/forward_parts/pallas_call | solution.py:110
  77.0 1.1 copy-done.1
  78.2 4.9 %all-to-all-start.1 = ((bf16[8,32,3072]{2,1,0:T(8,128)(2,1)}), bf16[8,32,3072]{2,1,0:T(8,128)(2,1)}, u32[]{:S(2)}, u32[]{:S(2)}) async-start(bf16[8,32,3072]{2,1,0:T(8,128)(2,1)} %bitcast.45), calls=%async_computation.1 | async-start | bytes 3145728 | tf_op jit(solution)/shard_map/all_to_all | solution.py:223
  83.0 0.8 fusion.11
  83.8 0.1 pad_maximum_fusion.3
  83.9 1.9 collective-permute-start.5
  85.8 1.9 collective-permute-done.5
  87.7 0.7 fusion.14
  88.5 4.2 %collective-permute-start.6 = (bf16[512,512]{1,0:T(8,128)(2,1)S(1)}, bf16[512,512]{1,0:T(8,128)(2,1)S(1)}, u32[]{:S(2)}, u32[]{:S(2)}) collective-permute-start(bf16[512,512]{1,0:T(8,128)(2,1)S(1)} %pad_maximum_fusion.4.token_pair), channel_id=1, source_target_pairs={{0,16},{16,0},{1,17},{17,1},{2,18},{18,2},{3,19},{19,3},{4,20},{20... | collective-permute-start | bytes 1572872 | tf_op jit(solution)/shard_map/ppermute | solution.py:50
  92.7 10.9 %all-to-all-done.1.arrived = bf16[8,32,3072]{2,1,0:T(8,128)(2,1)} async-done(((bf16[8,32,3072]{2,1,0:T(8,128)(2,1)}), bf16[8,32,3072]{2,1,0:T(8,128)(2,1)}, u32[]{:S(2)}, u32[]{:S(2)}) %all-to-all-start.1) | async-done | bytes 1572896 | tf_op jit(solution)/shard_map/all_to_all | solution.py:223
  103.6 2.4 %plane_parts.1 = (bf16[8,32,1024]{2,1,0:T(8,128)(2,1)}, bf16[32,1024]{1,0:T(8,128)(2,1)S(1)}, bf16[32,1024]{1,0:T(8,128)(2,1)S(1)}) custom-call(bf16[8,32,3072]{2,1,0:T(8,128)(2,1)} %all-to-all-done.1.arrived), custom_call_target="tpu_custom_call" | custom-call | tf_op jit(solution)/shard_map/plane_parts/pallas_call | solution.py:144
  105.9 4.5 %all-to-all-start.2 = ((bf16[8,32,1024]{2,1,0:T(8,128)(2,1)}), bf16[8,32,1024]{2,1,0:T(8,128)(2,1)S(1)}, u32[]{:S(2)}, u32[]{:S(2)}) async-start(bf16[8,32,1024]{2,1,0:T(8,128)(2,1)} %get-tuple-element.39), calls=%async_computation.2 | async-start | bytes 1048576 | tf_op jit(solution)/shard_map/all_to_all | solution.py:229
  110.5 0.8 slice_bitcast_fusion.1
  111.3 4.2 %collective-permute-start.4 = (bf16[32,1024]{1,0:T(8,128)(2,1)S(1)}, bf16[32,1024]{1,0:T(8,128)(2,1)S(1)}, u32[]{:S(2)}, u32[]{:S(2)}) collective-permute-start(bf16[32,1024]{1,0:T(8,128)(2,1)S(1)} %get-tuple-element.38), channel_id=1, source_target_pairs={{0,16},{16,0},{1,17},{17,1},{2,18},{18,2},{3,19},{19,3},{4,20},{20... | collective-permute-start | bytes 196616 | tf_op jit(solution)/shard_map/ppermute | solution.py:50
  115.5 1.9 slice_bitcast_fusion
  117.4 0.0 collective-permute-done.6.token_far
  117.4 4.1 %collective-permute-done.4 = bf16[32,1024]{1,0:T(8,128)(2,1)S(1)} collective-permute-done((bf16[32,1024]{1,0:T(8,128)(2,1)S(1)}, bf16[32,1024]{1,0:T(8,128)(2,1)S(1)}, u32[]{:S(2)}, u32[]{:S(2)}) %collective-permute-start.4) | collective-permute-done | bytes 65568 | tf_op jit(solution)/shard_map/ppermute | solution.py:50
  121.4 0.0 all-to-all-done.2
  121.4 1.9 collective-permute-start.7
  123.4 1.1 broadcast_in_dim.5
  124.5 4.8 %all-to-all-start.3 = ((bf16[8,2,32,1024]{3,2,1,0:T(8,128)(2,1)}), bf16[8,2,32,1024]{3,2,1,0:T(8,128)(2,1)S(1)}, u32[]{:S(2)}, u32[]{:S(2)}) async-start(bf16[8,2,32,1024]{3,2,1,0:T(8,128)(2,1)} %broadcast_in_dim.5), calls=%async_computation.3 | async-start | bytes 2097152 | tf_op jit(solution)/shard_map/all_to_all | solution.py:85
  129.3 1.6 convolution_convert_fusion.1
  131.0 0.0 copy-start.8
  131.0 0.0 copy-start.9
  131.0 0.0 collective-permute-done.7
  131.0 1.9 fusion.13
  132.9 0.8 pad_maximum_fusion.7
  133.7 4.5 %collective-permute-start.9 = (bf16[512,512]{1,0:T(8,128)(2,1)}, bf16[512,512]{1,0:T(8,128)(2,1)}, u32[]{:S(2)}, u32[]{:S(2)}) collective-permute-start(bf16[512,512]{1,0:T(8,128)(2,1)} %pad_maximum_fusion.7), channel_id=1, source_target_pairs={{0,16},{16,0},{1,17},{17,1},{2,18},{18,2},{3,19},{19,3},{4,20},{20... | collective-permute-start | bytes 1572872 | tf_op jit(solution)/shard_map/ppermute | solution.py:50
  138.3 1.5 convolution_convert_fusion
  139.7 0.1 pad_maximum_fusion.5
  139.8 0.7 dynamic-slice_bitcast_fusion
  140.5 2.2 %collective-permute-start.8 = (bf16[8,32,512]{2,1,0:T(8,128)(2,1)}, bf16[8,32,512]{2,1,0:T(8,128)(2,1)}, u32[]{:S(2)}, u32[]{:S(2)}) collective-permute-start(bf16[8,32,512]{2,1,0:T(8,128)(2,1)} %dynamic-slice_bitcast_fusion), channel_id=1, source_target_pairs={{0,1},{1,0},{2,3},{3,2},{4,5},{5,4},{6,7},{7,6},{8,9},{9,8},{10,11... | collective-permute-start | bytes 786440 | tf_op jit(solution)/shard_map/ppermute | solution.py:80
  142.8 0.8 pad_maximum_fusion.6
  143.6 7.0 %collective-permute-done.8 = bf16[8,32,512]{2,1,0:T(8,128)(2,1)} collective-permute-done((bf16[8,32,512]{2,1,0:T(8,128)(2,1)}, bf16[8,32,512]{2,1,0:T(8,128)(2,1)}, u32[]{:S(2)}, u32[]{:S(2)}) %collective-permute-start.8) | collective-permute-done | bytes 262176 | tf_op jit(solution)/shard_map/ppermute | solution.py:80
  150.6 1.7 fusion.3
  152.3 0.0 all-to-all-done.3.own
  152.3 3.4 %collective-permute-done.9 = bf16[512,512]{1,0:T(8,128)(2,1)} collective-permute-done((bf16[512,512]{1,0:T(8,128)(2,1)}, bf16[512,512]{1,0:T(8,128)(2,1)}, u32[]{:S(2)}, u32[]{:S(2)}) %collective-permute-start.9) | collective-permute-done | bytes 524320 | tf_op jit(solution)/shard_map/ppermute | solution.py:50
  155.8 1.9 collective-permute-start.10
  157.7 9.2 %all-to-all-start.4 = ((bf16[8,32,512]{2,1,0:T(8,128)(2,1)}), bf16[8,32,512]{2,1,0:T(8,128)(2,1)}, u32[]{:S(2)}, u32[]{:S(2)}) async-start(bf16[8,32,512]{2,1,0:T(8,128)(2,1)} %fusion.3), calls=%async_computation.4 | async-start | bytes 524288 | tf_op jit(solution)/shard_map/all_to_all | solution.py:247
  166.9 3.0 %collective-permute-start.11 = (bf16[512,512]{1,0:T(8,128)(2,1)}, bf16[512,512]{1,0:T(8,128)(2,1)}, u32[]{:S(2)}, u32[]{:S(2)}) collective-permute-start(bf16[512,512]{1,0:T(8,128)(2,1)} %pad_maximum_fusion.6), channel_id=1, source_target_pairs={{0,16},{16,0},{1,17},{17,1},{2,18},{18,2},{3,19},{19,3},{4,20},{20... | collective-permute-start | bytes 1572872 | tf_op jit(solution)/shard_map/ppermute | solution.py:50
  169.9 0.0 collective-permute-done.10.other
  169.9 2.4 %pair_grads.1 = (f32[512,512]{1,0:T(8,128)}, f32[512,512]{1,0:T(8,128)}) custom-call(bf16[512,512]{1,0:T(8,128)(2,1)S(1)} %pad_maximum_fusion.4.token_pair, bf16[512,512]{1,0:T(8,128)(2,1)S(1)} %copy-done.3, bf16[8,2,32,1024]{3,2,1,0:T(8,128)(2,1)S(1)} %all-to-all-done.3.own, bf16[8,2,32,1024]{3,2,1,0:T(8,128)(2,1)S(1)} %collective-permute-done.10.other), custom_call_target="tpu_custom_call" | custom-call | flops 1073741824 | bytes 5242880 | tf_op jit(solution)/shard_map/pair_grads/pallas_call | solution.py:176
  172.3 15.8 %all-to-all-done.4 = bf16[8,32,512]{2,1,0:T(8,128)(2,1)} async-done(((bf16[8,32,512]{2,1,0:T(8,128)(2,1)}), bf16[8,32,512]{2,1,0:T(8,128)(2,1)}, u32[]{:S(2)}, u32[]{:S(2)}) %all-to-all-start.4) | async-done | bytes 262176 | tf_op jit(solution)/shard_map/all_to_all | solution.py:247
  188.1 1.0 convert_reduce_fusion
  189.1 0.6 fusion.4
  189.7 0.0 collective-permute-done.11
  189.7 1.7 fusion.15
  191.4 0.0 copy-done.4
  191.4 1.4 convolution_add_fusion
  (28 shorter events, 0.2 us)
Async XLA Ops:
  1.2 10.8 %copy-start.10 = (bf16[32,512]{1,0:T(8,128)(2,1)S(1)}, bf16[32,512]{1,0:T(8,128)(2,1)}, u32[]{:S(2)}) copy-start(bf16[32,512]{1,0:T(8,128)(2,1)} %param.8) | copy-start | bytes 98308
  1.2 10.8 %copy-start.11 = (bf16[32,512]{1,0:T(8,128)(2,1)S(1)}, bf16[32,512]{1,0:T(8,128)(2,1)}, u32[]{:S(2)}) copy-start(bf16[32,512]{1,0:T(8,128)(2,1)} %param.9) | copy-start | bytes 98308
  5.1 68.0 %copy-start = (bf16[3,512,512]{2,1,0:T(8,128)(2,1)S(1)}, bf16[3,512,512]{2,1,0:T(8,128)(2,1)}, u32[]{:S(2)}) copy-start(bf16[3,512,512]{2,1,0:T(8,128)(2,1)} %dequantize.1.near) | copy-start | bytes 4718596
  5.1 62.5 %collective-permute-start = (bf16[3,512,512]{2,1,0:T(8,128)(2,1)}, bf16[3,512,512]{2,1,0:T(8,128)(2,1)}, u32[]{:S(2)}, u32[]{:S(2)}) collective-permute-start(bf16[3,512,512]{2,1,0:T(8,128)(2,1)} %dequantize.1.near), channel_id=1, source_target_pairs={{0,16},{16,0},{1,17},{17,1},{2,18},{18,2},{3,19},{19,3},{4,20},{20... | collective-permute-start | bytes 4718600 | tf_op jit(solution)/shard_map/ppermute | solution.py:50
  10.1 59.3 %collective-permute-start.2 = (bf16[3,512,512]{2,1,0:T(8,128)(2,1)}, bf16[3,512,512]{2,1,0:T(8,128)(2,1)}, u32[]{:S(2)}, u32[]{:S(2)}) collective-permute-start(bf16[3,512,512]{2,1,0:T(8,128)(2,1)} %dequantize.1.near), channel_id=1, source_target_pairs={{0,32},{32,0},{1,33},{33,1},{2,34},{34,2},{3,35},{35,3},{4,36},{36... | collective-permute-start | bytes 4718600 | tf_op jit(solution)/shard_map/ppermute | solution.py:50
  12.1 3.4 %collective-permute-start.1 = (bf16[2,16,512]{2,1,0:T(8,128)(2,1)S(1)}, bf16[2,16,512]{2,1,0:T(8,128)(2,1)S(1)}, u32[]{:S(2)}, u32[]{:S(2)}) collective-permute-start(bf16[2,16,512]{2,1,0:T(8,128)(2,1)S(1)} %get-tuple-element.66), channel_id=1, source_target_pairs={{0,32},{32,0},{1,33},{33,1},{2,34},{34,2},{3,35},{35,3},{4,36},{36... | collective-permute-start | bytes 98312 | tf_op jit(solution)/shard_map/ppermute | solution.py:50
  16.1 51.4 %all-to-all-start = ((bf16[16,16,128]{2,1,0:T(8,128)(2,1)}), bf16[16,16,128]{2,1,0:T(8,128)(2,1)S(1)}, u32[]{:S(2)}, u32[]{:S(2)}) async-start(bf16[16,16,128]{2,1,0:T(8,128)(2,1)} %broadcast_in_dim.4), calls=%async_computation | async-start | bytes 131072 | tf_op jit(solution)/shard_map/all_to_all | solution.py:215
  67.5 5.5 %collective-permute-start.3 = (bf16[3,512,512]{2,1,0:T(8,128)(2,1)}, bf16[3,512,512]{2,1,0:T(8,128)(2,1)S(1)}, u32[]{:S(2)}, u32[]{:S(2)}) collective-permute-start(bf16[3,512,512]{2,1,0:T(8,128)(2,1)} %collective-permute-done.far), channel_id=1, source_target_pairs={{0,32},{32,0},{1,33},{33,1},{2,34},{34,2},{3,35},{35,3},{4,36},{36... | collective-permute-start | bytes 4718600 | tf_op jit(solution)/shard_map/ppermute | solution.py:50
  77.0 1.1 copy-start.1
  78.2 25.4 %all-to-all-start.1 = ((bf16[8,32,3072]{2,1,0:T(8,128)(2,1)}), bf16[8,32,3072]{2,1,0:T(8,128)(2,1)}, u32[]{:S(2)}, u32[]{:S(2)}) async-start(bf16[8,32,3072]{2,1,0:T(8,128)(2,1)} %bitcast.45), calls=%async_computation.1 | async-start | bytes 3145728 | tf_op jit(solution)/shard_map/all_to_all | solution.py:223
  83.9 3.8 %collective-permute-start.5 = (bf16[256,1024]{1,0:T(8,128)(2,1)S(1)}, bf16[256,1024]{1,0:T(8,128)(2,1)S(1)}, u32[]{:S(2)}, u32[]{:S(2)}) collective-permute-start(bf16[256,1024]{1,0:T(8,128)(2,1)S(1)} %pad_maximum_fusion.3), channel_id=1, source_target_pairs={{0,32},{32,0},{1,33},{33,1},{2,34},{34,2},{3,35},{35,3},{4,36},{36... | collective-permute-start | bytes 1572872 | tf_op jit(solution)/shard_map/ppermute | solution.py:50
  88.5 28.9 %collective-permute-start.6 = (bf16[512,512]{1,0:T(8,128)(2,1)S(1)}, bf16[512,512]{1,0:T(8,128)(2,1)S(1)}, u32[]{:S(2)}, u32[]{:S(2)}) collective-permute-start(bf16[512,512]{1,0:T(8,128)(2,1)S(1)} %pad_maximum_fusion.4.token_pair), channel_id=1, source_target_pairs={{0,16},{16,0},{1,17},{17,1},{2,18},{18,2},{3,19},{19,3},{4,20},{20... | collective-permute-start | bytes 1572872 | tf_op jit(solution)/shard_map/ppermute | solution.py:50
  105.9 15.5 %all-to-all-start.2 = ((bf16[8,32,1024]{2,1,0:T(8,128)(2,1)}), bf16[8,32,1024]{2,1,0:T(8,128)(2,1)S(1)}, u32[]{:S(2)}, u32[]{:S(2)}) async-start(bf16[8,32,1024]{2,1,0:T(8,128)(2,1)} %get-tuple-element.39), calls=%async_computation.2 | async-start | bytes 1048576 | tf_op jit(solution)/shard_map/all_to_all | solution.py:229
  111.3 10.1 %collective-permute-start.4 = (bf16[32,1024]{1,0:T(8,128)(2,1)S(1)}, bf16[32,1024]{1,0:T(8,128)(2,1)S(1)}, u32[]{:S(2)}, u32[]{:S(2)}) collective-permute-start(bf16[32,1024]{1,0:T(8,128)(2,1)S(1)} %get-tuple-element.38), channel_id=1, source_target_pairs={{0,16},{16,0},{1,17},{17,1},{2,18},{18,2},{3,19},{19,3},{4,20},{20... | collective-permute-start | bytes 196616 | tf_op jit(solution)/shard_map/ppermute | solution.py:50
  117.4 7.1 %copy-start.2 = (bf16[512,512]{1,0:T(8,128)(2,1)}, bf16[512,512]{1,0:T(8,128)(2,1)S(1)}, u32[]{:S(2)}) copy-start(bf16[512,512]{1,0:T(8,128)(2,1)S(1)} %collective-permute-done.6.token_far) | copy-start | bytes 1572868
  121.4 9.6 %collective-permute-start.7 = (bf16[256,1024]{1,0:T(8,128)(2,1)S(1)}, bf16[256,1024]{1,0:T(8,128)(2,1)}, u32[]{:S(2)}, u32[]{:S(2)}) collective-permute-start(bf16[256,1024]{1,0:T(8,128)(2,1)S(1)} %bitcast.49), channel_id=1, source_target_pairs={{0,32},{32,0},{1,33},{33,1},{2,34},{34,2},{3,35},{35,3},{4,36},{36... | collective-permute-start | bytes 1572872 | tf_op jit(solution)/shard_map/ppermute | solution.py:50
  124.5 27.9 %all-to-all-start.3 = ((bf16[8,2,32,1024]{3,2,1,0:T(8,128)(2,1)}), bf16[8,2,32,1024]{3,2,1,0:T(8,128)(2,1)S(1)}, u32[]{:S(2)}, u32[]{:S(2)}) async-start(bf16[8,2,32,1024]{3,2,1,0:T(8,128)(2,1)} %broadcast_in_dim.5), calls=%async_computation.3 | async-start | bytes 2097152 | tf_op jit(solution)/shard_map/all_to_all | solution.py:85
  131.0 7.3 %copy-start.8 = (bf16[512,512]{1,0:T(8,128)(2,1)S(1)}, bf16[512,512]{1,0:T(8,128)(2,1)}, u32[]{:S(2)}) copy-start(bf16[512,512]{1,0:T(8,128)(2,1)} %slice_bitcast_fusion.1) | copy-start | bytes 1572868
  131.0 7.3 %copy-start.9 = (bf16[512,512]{1,0:T(8,128)(2,1)S(1)}, bf16[512,512]{1,0:T(8,128)(2,1)}, u32[]{:S(2)}) copy-start(bf16[512,512]{1,0:T(8,128)(2,1)} %slice_bitcast_fusion) | copy-start | bytes 1572868
  133.7 9.1 %copy-start.6 = (bf16[256,512]{1,0:T(8,128)(2,1)S(1)}, bf16[256,512]{1,0:T(8,128)(2,1)}, u32[]{:S(2)}) copy-start(bf16[256,512]{1,0:T(8,128)(2,1)} %get-tuple-element.56) | copy-start | bytes 786436
  133.7 9.1 %copy-start.7 = (bf16[256,512]{1,0:T(8,128)(2,1)S(1)}, bf16[256,512]{1,0:T(8,128)(2,1)}, u32[]{:S(2)}) copy-start(bf16[256,512]{1,0:T(8,128)(2,1)} %get-tuple-element.63) | copy-start | bytes 786436
  133.7 22.1 %collective-permute-start.9 = (bf16[512,512]{1,0:T(8,128)(2,1)}, bf16[512,512]{1,0:T(8,128)(2,1)}, u32[]{:S(2)}, u32[]{:S(2)}) collective-permute-start(bf16[512,512]{1,0:T(8,128)(2,1)} %pad_maximum_fusion.7), channel_id=1, source_target_pairs={{0,16},{16,0},{1,17},{17,1},{2,18},{18,2},{3,19},{19,3},{4,20},{20... | collective-permute-start | bytes 1572872 | tf_op jit(solution)/shard_map/ppermute | solution.py:50
  139.8 30.1 %copy-start.3 = (bf16[512,512]{1,0:T(8,128)(2,1)S(1)}, bf16[512,512]{1,0:T(8,128)(2,1)}, u32[]{:S(2)}) copy-start(bf16[512,512]{1,0:T(8,128)(2,1)} %copy-done.2) | copy-start | bytes 1572868
  140.5 10.1 %collective-permute-start.8 = (bf16[8,32,512]{2,1,0:T(8,128)(2,1)}, bf16[8,32,512]{2,1,0:T(8,128)(2,1)}, u32[]{:S(2)}, u32[]{:S(2)}) collective-permute-start(bf16[8,32,512]{2,1,0:T(8,128)(2,1)} %dynamic-slice_bitcast_fusion), channel_id=1, source_target_pairs={{0,1},{1,0},{2,3},{3,2},{4,5},{5,4},{6,7},{7,6},{8,9},{9,8},{10,11... | collective-permute-start | bytes 786440 | tf_op jit(solution)/shard_map/ppermute | solution.py:80
  155.8 14.1 %collective-permute-start.10 = (bf16[8,2,32,1024]{3,2,1,0:T(8,128)(2,1)S(1)}, bf16[8,2,32,1024]{3,2,1,0:T(8,128)(2,1)S(1)}, u32[]{:S(2)}, u32[]{:S(2)}) collective-permute-start(bf16[8,2,32,1024]{3,2,1,0:T(8,128)(2,1)S(1)} %all-to-all-done.3.own), channel_id=1, source_target_pairs={{0,32},{32,0},{1,33},{33,1},{2,34},{34,2},{3,35},{35,3},{4,36},{36... | collective-permute-start | bytes 3145736 | tf_op jit(solution)/shard_map/ppermute | solution.py:50
  157.7 30.4 %all-to-all-start.4 = ((bf16[8,32,512]{2,1,0:T(8,128)(2,1)}), bf16[8,32,512]{2,1,0:T(8,128)(2,1)}, u32[]{:S(2)}, u32[]{:S(2)}) async-start(bf16[8,32,512]{2,1,0:T(8,128)(2,1)} %fusion.3), calls=%async_computation.4 | async-start | bytes 524288 | tf_op jit(solution)/shard_map/all_to_all | solution.py:247
  166.9 22.8 %collective-permute-start.11 = (bf16[512,512]{1,0:T(8,128)(2,1)}, bf16[512,512]{1,0:T(8,128)(2,1)}, u32[]{:S(2)}, u32[]{:S(2)}) collective-permute-start(bf16[512,512]{1,0:T(8,128)(2,1)} %pad_maximum_fusion.6), channel_id=1, source_target_pairs={{0,16},{16,0},{1,17},{17,1},{2,18},{18,2},{3,19},{19,3},{4,20},{20... | collective-permute-start | bytes 1572872 | tf_op jit(solution)/shard_map/ppermute | solution.py:50
  172.3 19.1 %copy-start.4 = (bf16[512,512]{1,0:T(8,128)(2,1)S(1)}, bf16[512,512]{1,0:T(8,128)(2,1)}, u32[]{:S(2)}) copy-start(bf16[512,512]{1,0:T(8,128)(2,1)} %pad_maximum_fusion.6) | copy-start | bytes 1572868
  172.3 19.1 %copy-start.5 = (bf16[256,512]{1,0:T(8,128)(2,1)S(1)}, bf16[256,512]{1,0:T(8,128)(2,1)}, u32[]{:S(2)}) copy-start(bf16[256,512]{1,0:T(8,128)(2,1)} %get-tuple-element.61) | copy-start | bytes 786436
